TPU v7x, 128 devices: a whole 4x4x4 slice. The times are simulated.
128 devices in a mesh: gx: 8 (over z, core), yz: 16 (over x, y).
Axes of the slice: x: 4, y: 4, z: 4, core: 2. Of those that a mesh axis runs over, the one named last changes fastest.
Arguments:
- starting_warmth_level: float32 [64, 128, 1024], P('gx', 'yz'), may hold values from -6 to 6
- diffusive_coefficient_map: float32 [64, 128, 1024], P('gx', 'yz'), may hold values from 0.5 to 8
- specific_warmth_store: float32 [64, 128, 1024], P('gx', 'yz'), may hold values from 0.25 to 2
- energy_source_flux: float32 [64, 128, 1024], P('gx', 'yz'), may hold values from -6 to 6
- deformation_vector: float32 [3, 64, 128, 1024], P(None, 'gx', 'yz'), may hold values from -6 to 6
- substance_label_columns: int32 [64, 128], P('gx'), may hold values from 0 to 1
- substance_moduli_table: float32 [2, 2], replicated, may hold values from 0.5 to 2
- subdomain_point_tally: int32 [16], replicated, may hold values from 1 to 128, 1024 in all
Outputs:
- final_warmth_level: float32 [64, 128, 1024], P('gx', 'yz')
- residual: float32 [3, 64, 128, 2048], P(None, 'gx', None, 'yz')
Inputs may be any that keep to these rules, and one draw needn't show every extreme that they name: `subdomain_point_tally`: the lengths sum to 1024, and some part has exactly 128 nodes.
All inputs are finite; a program needn't handle non-finite values.
Results may differ from a plain program's by a relative error of at most 0.00026.
Values sent between devices are 32-bit elements; how exact they have to be, the bound alone decides.
A program may use at most 128 MiB of HBM per device.

v0:
```python
import jax
import jax.numpy as jnp
from jax import lax
from jax.sharding import PartitionSpec as P

NCHEB = 6
STEPS = 2
NMAT = 2
ZMAX = 128


time_step = 1.0


def extended(value, sides, width):
    for axis, dim in sides:
        devices, length = (lax.axis_size(axis), value.shape[dim])
        up = [(i, (i + 1) % devices) for i in range(devices - 1)]
        down = [(j, i) for i, j in up]
        last = lax.slice_in_dim(value, length - width, length, axis=dim)
        initial = lax.slice_in_dim(value, 0, width, axis=dim)
        before = lax.ppermute(last, axis, up)
        after = lax.ppermute(initial, axis, down)
        value = jnp.concatenate([before, value, after], axis=dim)
    return value


def from_behind(value, axis, steps):
    count = lax.axis_size(axis)
    initial, last = (max(0, -steps), min(count, count - steps))
    return lax.ppermute(value, axis, [(source, source + steps) for source in range(initial, last)])


def harmonic(first, second):
    return 2.0 * first * second / (first + second)


def neighbours(padded_field):
    return [
        padded_field[2:, 1:-1, 1:-1],
        padded_field[:-2, 1:-1, 1:-1],
        padded_field[1:-1, 2:, 1:-1],
        padded_field[1:-1, :-2, 1:-1],
        padded_field[1:-1, 1:-1, 2:],
        padded_field[1:-1, 1:-1, :-2],
    ]


def apply_heat(field, coefs, specific_warmth_store):
    bordered = extended(field, (("gx", 0), ("yz", 1)), 1)
    beside_all = neighbours(jnp.pad(bordered, ((0, 0), (0, 0), (1, 1))))
    total = jnp.zeros_like(field)
    for coef, other in zip(coefs, beside_all):
        total = total + coef * (field - other)
    return specific_warmth_store * field + time_step * total


def chebyshev(rhs, start, coefs, specific_warmth_store, low, high):
    theta = (high + low) / 2.0
    delta = (high - low) / 2.0
    sigma = theta / delta
    rho = 1.0 / sigma
    solution = start
    resid = rhs - apply_heat(solution, coefs, specific_warmth_store)
    direction = resid / theta
    for turn in range(NCHEB):
        solution = solution + direction
        resid = resid - apply_heat(direction, coefs, specific_warmth_store)
        rho_new = 1.0 / (2.0 * sigma - rho)
        direction = rho_new * rho * direction + 2.0 * rho_new / delta * resid
        rho = rho_new
    return solution


def lookup(substance_label_columns, row):
    total = jnp.zeros(substance_label_columns.shape, jnp.float32)
    for index in range(NMAT):
        total = total + jnp.where(substance_label_columns == index, row[index], 0.0)
    return total


def combine_residual(fields, plus_minus, shear):
    parts = []
    for comp in range(3):
        lap = 6.0 * fields[comp]
        for plus, minus in plus_minus:
            lap = lap - plus[comp] - minus[comp]
        upper, lower = plus_minus[comp]
        parts.append(shear * lap + 0.5 * (upper[3] - lower[3]))
    return jnp.stack(parts, 0)


def local(
    starting_warmth_level,
    diffusive_coefficient_map,
    specific_warmth_store,
    energy_source_flux,
    deformation_vector,
    substance_label_columns,
    substance_moduli_table,
    subdomain_point_tally,
):
    kborder = extended(diffusive_coefficient_map, (("gx", 0), ("yz", 1)), 1)
    coefs = [
        harmonic(diffusive_coefficient_map, other)
        for other in neighbours(jnp.pad(kborder, ((0, 0), (0, 0), (1, 1))))
    ]
    summed = coefs[0] + coefs[1] + coefs[2] + coefs[3] + coefs[4] + coefs[5]
    upper_local = jnp.max(specific_warmth_store + 2.0 * time_step * summed)
    lower_local = jnp.min(specific_warmth_store)
    high = lax.pmax(upper_local, ("gx", "yz"))
    low = lax.pmin(lower_local, ("gx", "yz"))
    final_warmth_level = starting_warmth_level
    for step in range(STEPS):
        rhs = specific_warmth_store * final_warmth_level + time_step * energy_source_flux
        final_warmth_level = chebyshev(
            rhs, final_warmth_level, coefs, specific_warmth_store, low, high
        )
    shear_col = lookup(substance_label_columns, substance_moduli_table[0])
    beta_col = lookup(substance_label_columns, substance_moduli_table[1])
    column = lax.axis_index("yz")
    starts = jnp.cumsum(subdomain_point_tally) - subdomain_point_tally
    offsets = jnp.arange(ZMAX, dtype=jnp.int32)
    where_from = (starts[:, None] + offsets[None, :]).reshape(-1)
    valid = (offsets[None, :] < subdomain_point_tally[:, None]).reshape(-1).astype(jnp.float32)
    padded_field = jnp.pad(
        jnp.concatenate([final_warmth_level[None], deformation_vector], 0),
        ((0, 0), (0, 0), (0, 0), (0, ZMAX)),
    )
    sent = jnp.take(padded_field, where_from, axis=3) * valid
    arrived = lax.all_to_all(sent, "yz", split_axis=3, concat_axis=2, tiled=True)
    stress = beta_col[:, :, None] * arrived[0]
    fields = jnp.concatenate([arrived[1:4], stress[None]], 0)
    length = subdomain_point_tally[column]
    xborder = extended(fields, (("gx", 1),), 1)
    zero_y = jnp.zeros_like(fields[:, :, :1])
    y_plus = jnp.concatenate([fields[:, :, 1:], zero_y], 2)
    y_minus = jnp.concatenate([zero_y, fields[:, :, :-1]], 2)
    next_plane = from_behind(fields[:, :, :, 0], "yz", -1)
    last_plane = lax.dynamic_index_in_dim(fields, length - 1, 3, keepdims=False)
    prev_plane = from_behind(last_plane, "yz", 1)
    empty_third_plane = jnp.zeros_like(fields[..., :1])
    z_plus = jnp.where(
        offsets == length - 1,
        next_plane[..., None],
        jnp.concatenate([fields[..., 1:], empty_third_plane], 3),
    )
    z_minus = jnp.where(
        offsets == 0,
        prev_plane[..., None],
        jnp.concatenate([empty_third_plane, fields[..., :-1]], 3),
    )
    plus_minus = [(xborder[:, 2:], xborder[:, :-2]), (y_plus, y_minus), (z_plus, z_minus)]
    result = combine_residual(fields, plus_minus, shear_col[:, :, None])
    residual = result * (offsets < length).astype(jnp.float32)
    return (final_warmth_level, residual)


def solution(mesh):
    placed = (
        P("gx", "yz", None),
        P("gx", "yz", None),
        P("gx", "yz", None),
        P("gx", "yz", None),
        P(None, "gx", "yz", None),
        P("gx", None),
        P(),
        P(),
    )
    return jax.shard_map(
        local,
        mesh=mesh,
        in_specs=placed,
        out_specs=(P("gx", "yz", None), P(None, "gx", None, "yz")),
        check_vma=False,
    )
```

profile of v0, /device:TPU:1, one launch (start us, length us, event | category | flops | bytes accessed | tf_op | source)
XLA Modules:
  0.0 596.0 jit_solution(10760630004475913047)
XLA Ops:
  1.5 4.9 collective-permute-start.2
  9.1 3.6 collective-permute-start.3
  12.8 1.9 collective-permute-start.1
  17.1 4.0 collective-permute-start.6
  23.5 4.0 collective-permute-start.7
  29.0 71.0 %pmax.7 = f32[]{:T(128)} all-reduce(f32[]{:T(128)} %get-tuple-element.9), channel_id=1, replica_groups=mesh['gx'=8,'yz'=16] {'gx','yz'}, use_global_device_ids=true, to_apply=%region_1.2 | all-reduce | flops 1 | bytes 8 | tf_op jit(solution)/shard_map/pmax | solution.py:111
  100.0 63.2 %pmin.7 = f32[]{:T(128)} all-reduce(f32[]{:T(128)} %get-tuple-element.8), channel_id=1, replica_groups=mesh['gx'=8,'yz'=16] {'gx','yz'}, use_global_device_ids=true, to_apply=%region_3.4 | all-reduce | flops 1 | bytes 8 | tf_op jit(solution)/shard_map/pmin | solution.py:112
  166.5 2.6 collective-permute-start.8
  169.0 3.0 collective-permute-start.9
  174.4 4.0 collective-permute-start.11
  180.7 2.2 collective-permute-start.12
  183.0 4.7 collective-permute-start.13
  190.0 4.6 collective-permute-start.15
  198.6 5.1 collective-permute-start.17
  206.0 4.6 collective-permute-start.19
  213.6 1.9 collective-permute-start.20
  215.5 5.1 collective-permute-start.21
  223.0 4.6 collective-permute-start.23
  229.2 2.0 multiply_add_fusion.4
  233.1 5.1 collective-permute-start.25
  240.6 4.8 collective-permute-start.27
  248.9 1.9 collective-permute-start.28
  250.8 5.1 collective-permute-start.29
  258.2 7.2 %collective-permute-start.31 = (f32[10,1,1024]{2,1,0:T(1,128)S(1)}, f32[10,1,1024]{2,1,0:T(1,128)S(1)}, u32[]{:S(2)}, u32[]{:S(2)}) collective-permute-start(f32[10,1,1024]{2,1,0:T(1,128)S(1)} %get-tuple-element.49), channel_id=1, source_target_pairs={{0,1},{1,2},{2,3},{3,4},{4,5},{5,6},{6,7},{7,8},{8,9},{9,10},{10,1... | collective-permute-start | bytes 122888 | tf_op jit(solution)/shard_map/ppermute | solution.py:22
  266.9 1.9 collective-permute-start.32
  268.8 5.1 collective-permute-start.33
  276.3 6.7 %collective-permute-start.35 = (f32[10,1,1024]{2,1,0:T(1,128)S(1)}, f32[10,1,1024]{2,1,0:T(1,128)S(1)}, u32[]{:S(2)}, u32[]{:S(2)}) collective-permute-start(f32[10,1,1024]{2,1,0:T(1,128)S(1)} %get-tuple-element.47), channel_id=1, source_target_pairs={{0,1},{1,2},{2,3},{3,4},{4,5},{5,6},{6,7},{7,8},{8,9},{9,10},{10,1... | collective-permute-start | bytes 122888 | tf_op jit(solution)/shard_map/ppermute | solution.py:22
  286.9 5.1 collective-permute-start.37
  294.3 6.7 %collective-permute-start.39 = (f32[10,1,1024]{2,1,0:T(1,128)S(1)}, f32[10,1,1024]{2,1,0:T(1,128)S(1)}, u32[]{:S(2)}, u32[]{:S(2)}) collective-permute-start(f32[10,1,1024]{2,1,0:T(1,128)S(1)} %get-tuple-element.45), channel_id=1, source_target_pairs={{0,1},{1,2},{2,3},{3,4},{4,5},{5,6},{6,7},{7,8},{8,9},{9,10},{10,1... | collective-permute-start | bytes 122888 | tf_op jit(solution)/shard_map/ppermute | solution.py:22
  306.3 5.1 collective-permute-start.41
  314.9 6.7 %collective-permute-start.43 = (f32[10,1,1024]{2,1,0:T(1,128)S(1)}, f32[10,1,1024]{2,1,0:T(1,128)S(1)}, u32[]{:S(2)}, u32[]{:S(2)}) collective-permute-start(f32[10,1,1024]{2,1,0:T(1,128)S(1)} %get-tuple-element.43), channel_id=1, source_target_pairs={{0,1},{1,2},{2,3},{3,4},{4,5},{5,6},{6,7},{7,8},{8,9},{9,10},{10,1... | collective-permute-start | bytes 122888 | tf_op jit(solution)/shard_map/ppermute | solution.py:22
  325.4 1.9 collective-permute-start.44
  327.4 5.1 collective-permute-start.45
  334.8 6.7 %collective-permute-start.47 = (f32[10,1,1024]{2,1,0:T(1,128)S(1)}, f32[10,1,1024]{2,1,0:T(1,128)S(1)}, u32[]{:S(2)}, u32[]{:S(2)}) collective-permute-start(f32[10,1,1024]{2,1,0:T(1,128)S(1)} %get-tuple-element.41), channel_id=1, source_target_pairs={{0,1},{1,2},{2,3},{3,4},{4,5},{5,6},{6,7},{7,8},{8,9},{9,10},{10,1... | collective-permute-start | bytes 122888 | tf_op jit(solution)/shard_map/ppermute | solution.py:22
  345.6 5.1 collective-permute-start.49
  353.0 6.7 %collective-permute-start.51 = (f32[10,1,1024]{2,1,0:T(1,128)S(1)}, f32[10,1,1024]{2,1,0:T(1,128)S(1)}, u32[]{:S(2)}, u32[]{:S(2)}) collective-permute-start(f32[10,1,1024]{2,1,0:T(1,128)S(1)} %get-tuple-element.39), channel_id=1, source_target_pairs={{0,1},{1,2},{2,3},{3,4},{4,5},{5,6},{6,7},{7,8},{8,9},{9,10},{10,1... | collective-permute-start | bytes 122888 | tf_op jit(solution)/shard_map/ppermute | solution.py:22
  363.2 8.6 %copy.196 = f32[4,8,8,1024]{2,1,3,0:T(8,128)} copy(f32[4,8,8,1024]{3,2,1,0:T(8,128)S(1)} %pad_maximum_fusion) | data formatting | bytes 2097152 | tf_op jit(solution)/shard_map/concatenate | solution.py:127
  371.8 12.6 %pad.61 = f32[4,8,8,1152]{2,1,3,0:T(8,128)} pad(f32[4,8,8,1024]{2,1,3,0:T(8,128)} %copy.196, f32[]{:T(128)} %constant.17.clone.1), padding=0_0x0_0x0_0x0_128 | pad | bytes 2228228 | tf_op jit(solution)/shard_map/jit(_pad)/pad | solution.py:126
  384.4 32.7 %gather_fusion = f32[2048,4,8,8]{3,2,1,0:T(8,128)} fusion(f32[4,8,8,1152]{2,1,3,0:T(8,128)} %pad.61, s32[2048]{0:T(1024)S(1)} %broadcast_clamp_fusion), kind=kCustom, calls=%fused_computation | custom fusion | bytes 4202496 | tf_op jit(solution)/shard_map/jit(_take)/gather | solution.py:130
  417.1 26.9 %fusion.281 = f32[2048,4,8,8]{3,2,1,0:T(8,128)} fusion(f32[2048]{0:T(1024)S(1)} %convert_bitcast_fusion, f32[2048,4,8,8]{3,2,1,0:T(8,128)} %gather_fusion, pred[2048]{0:T(1024)(128)(4,1)S(1)} %copy-done.25), kind=kLoop, calls=%fused_computation.554 | loop fusion | flops 1048576 | bytes 4204544
  443.9 24.3 %reshape.173 = f32[16,1,32768]{2,1,0:T(1,128)} reshape(f32[2048,4,8,8]{3,2,1,0:T(8,128)} %fusion.281) | data formatting | bytes 4194304
  468.2 15.3 %all-to-all-start = ((f32[16,1,32768]{2,1,0:T(1,128)}), f32[16,1,32768]{2,1,0:T(1,128)}, u32[]{:S(2)}, u32[]{:S(2)}) async-start(f32[16,1,32768]{2,1,0:T(1,128)} %reshape.173), calls=%async_computation | async-start | bytes 4194304 | tf_op jit(solution)/shard_map/all_to_all | solution.py:131
  489.3 23.7 %all-to-all-done = f32[16,1,32768]{2,1,0:T(1,128)} async-done(((f32[16,1,32768]{2,1,0:T(1,128)}), f32[16,1,32768]{2,1,0:T(1,128)}, u32[]{:S(2)}, u32[]{:S(2)}) %all-to-all-start) | async-done | bytes 2097184 | tf_op jit(solution)/shard_map/all_to_all | solution.py:131
  513.6 8.6 %reduce.5 = f32[16,32768]{1,0:T(8,128)} reduce(f32[16,1,32768]{2,1,0:T(1,128)} %all-to-all-done, f32[]{:T(128)} %broadcast.490), dimensions={1}, to_apply=%all_to_all.11.reduce_sub_computation | reduce | bytes 4194308 | tf_op jit(solution)/shard_map/all_to_all | solution.py:131
  522.2 32.1 %reshape.174 = f32[2048,4,8,8]{3,2,1,0:T(8,128)} reshape(f32[16,32768]{1,0:T(8,128)} %reduce.5) | data formatting | bytes 4194304
  554.3 20.3 %copy.197 = f32[4,8,8,16,128]{4,2,3,1,0:T(8,128)} copy(f32[4,8,8,16,128]{2,1,0,4,3:T(8,128)} %bitcast.42) | data formatting | bytes 4194304 | tf_op jit(solution)/shard_map/all_to_all | solution.py:131
  579.7 2.2 collective-permute-start.55
  583.9 4.1 collective-permute-start.53
  (226 shorter events, 94.4 us)
Async XLA Ops:
  1.5 13.2 %collective-permute-start.2 = (f32[1,8,1024]{2,1,0:T(8,128)S(1)}, f32[1,8,1024]{2,1,0:T(8,128)S(1)}, u32[]{:S(2)}, u32[]{:S(2)}) collective-permute-start(f32[1,8,1024]{2,1,0:T(8,128)S(1)} %get-tuple-element.90), channel_id=1, source_target_pairs={{0,16},{16,32},{32,48},{48,64},{64,80},{80,96},{96,112},{1,17},{17... | collective-permute-start | bytes 98312 | tf_op jit(solution)/shard_map/ppermute | solution.py:22
  6.4 9.3 %collective-permute-start = (f32[1,8,1024]{2,1,0:T(8,128)S(1)}, f32[1,8,1024]{2,1,0:T(8,128)S(1)}, u32[]{:S(2)}, u32[]{:S(2)}) collective-permute-start(f32[1,8,1024]{2,1,0:T(8,128)S(1)} %get-tuple-element.89), channel_id=1, source_target_pairs={{16,0},{32,16},{48,32},{64,48},{80,64},{96,80},{112,96},{17,1},{33... | collective-permute-start | bytes 98312 | tf_op jit(solution)/shard_map/ppermute | solution.py:23
  9.1 11.9 %collective-permute-start.3 = (f32[1,8,1024]{2,1,0:T(8,128)S(1)}, f32[1,8,1024]{2,1,0:T(8,128)S(1)}, u32[]{:S(2)}, u32[]{:S(2)}) collective-permute-start(f32[1,8,1024]{2,1,0:T(8,128)S(1)} %get-tuple-element.88), channel_id=1, source_target_pairs={{0,16},{16,32},{32,48},{48,64},{64,80},{80,96},{96,112},{1,17},{17... | collective-permute-start | bytes 98312 | tf_op jit(solution)/shard_map/ppermute | solution.py:22
  12.8 9.3 %collective-permute-start.1 = (f32[1,8,1024]{2,1,0:T(8,128)S(1)}, f32[1,8,1024]{2,1,0:T(8,128)S(1)}, u32[]{:S(2)}, u32[]{:S(2)}) collective-permute-start(f32[1,8,1024]{2,1,0:T(8,128)S(1)} %get-tuple-element.87), channel_id=1, source_target_pairs={{16,0},{32,16},{48,32},{64,48},{80,64},{96,80},{112,96},{17,1},{33... | collective-permute-start | bytes 98312 | tf_op jit(solution)/shard_map/ppermute | solution.py:23
  15.8 11.7 %collective-permute-start.4 = (f32[10,1,1024]{2,1,0:T(1,128)S(1)}, f32[10,1,1024]{2,1,0:T(1,128)S(1)}, u32[]{:S(2)}, u32[]{:S(2)}) collective-permute-start(f32[10,1,1024]{2,1,0:T(1,128)S(1)} %get-tuple-element.64), channel_id=1, source_target_pairs={{1,0},{2,1},{3,2},{4,3},{5,4},{6,5},{7,6},{8,7},{9,8},{10,9},{11,1... | collective-permute-start | bytes 122888 | tf_op jit(solution)/shard_map/ppermute | solution.py:23
  17.1 10.4 %collective-permute-start.6 = (f32[10,1,1024]{2,1,0:T(1,128)S(1)}, f32[10,1,1024]{2,1,0:T(1,128)S(1)}, u32[]{:S(2)}, u32[]{:S(2)}) collective-permute-start(f32[10,1,1024]{2,1,0:T(1,128)S(1)} %get-tuple-element.63), channel_id=1, source_target_pairs={{0,1},{1,2},{2,3},{3,4},{4,5},{5,6},{6,7},{7,8},{8,9},{9,10},{10,1... | collective-permute-start | bytes 122888 | tf_op jit(solution)/shard_map/ppermute | solution.py:22
  22.2 142.2 %collective-permute-start.5 = (f32[10,1,1024]{2,1,0:T(1,128)S(1)}, f32[10,1,1024]{2,1,0:T(1,128)S(1)}, u32[]{:S(2)}, u32[]{:S(2)}) collective-permute-start(f32[10,1,1024]{2,1,0:T(1,128)S(1)} %get-tuple-element.62), channel_id=1, source_target_pairs={{1,0},{2,1},{3,2},{4,3},{5,4},{6,5},{7,6},{8,7},{9,8},{10,9},{11,1... | collective-permute-start | bytes 122888 | tf_op jit(solution)/shard_map/ppermute | solution.py:23
  23.5 140.9 %collective-permute-start.7 = (f32[10,1,1024]{2,1,0:T(1,128)S(1)}, f32[10,1,1024]{2,1,0:T(1,128)S(1)}, u32[]{:S(2)}, u32[]{:S(2)}) collective-permute-start(f32[10,1,1024]{2,1,0:T(1,128)S(1)} %get-tuple-element.61), channel_id=1, source_target_pairs={{0,1},{1,2},{2,3},{3,4},{4,5},{5,6},{6,7},{7,8},{8,9},{9,10},{10,1... | collective-permute-start | bytes 122888 | tf_op jit(solution)/shard_map/ppermute | solution.py:22
  173.1 6.7 %collective-permute-start.10 = (f32[10,1,1024]{2,1,0:T(1,128)S(1)}, f32[10,1,1024]{2,1,0:T(1,128)S(1)}, u32[]{:S(2)}, u32[]{:S(2)}) collective-permute-start(f32[10,1,1024]{2,1,0:T(1,128)S(1)} %get-tuple-element.60), channel_id=1, source_target_pairs={{1,0},{2,1},{3,2},{4,3},{5,4},{6,5},{7,6},{8,7},{9,8},{10,9},{11,1... | collective-permute-start | bytes 122888 | tf_op jit(solution)/shard_map/ppermute | solution.py:23
  180.7 7.0 %collective-permute-start.12 = (f32[1,8,1024]{2,1,0:T(8,128)S(1)}, f32[1,8,1024]{2,1,0:T(8,128)S(1)}, u32[]{:S(2)}, u32[]{:S(2)}) collective-permute-start(f32[1,8,1024]{2,1,0:T(8,128)S(1)} %get-tuple-element.84), channel_id=1, source_target_pairs={{16,0},{32,16},{48,32},{64,48},{80,64},{96,80},{112,96},{17,1},{33... | collective-permute-start | bytes 98312 | tf_op jit(solution)/shard_map/ppermute | solution.py:23
  188.7 6.0 %collective-permute-start.14 = (f32[10,1,1024]{2,1,0:T(1,128)S(1)}, f32[10,1,1024]{2,1,0:T(1,128)S(1)}, u32[]{:S(2)}, u32[]{:S(2)}) collective-permute-start(f32[10,1,1024]{2,1,0:T(1,128)S(1)} %get-tuple-element.58), channel_id=1, source_target_pairs={{1,0},{2,1},{3,2},{4,3},{5,4},{6,5},{7,6},{8,7},{9,8},{10,9},{11,1... | collective-permute-start | bytes 122888 | tf_op jit(solution)/shard_map/ppermute | solution.py:23
  196.7 7.0 %collective-permute-start.16 = (f32[1,8,1024]{2,1,0:T(8,128)S(1)}, f32[1,8,1024]{2,1,0:T(8,128)S(1)}, u32[]{:S(2)}, u32[]{:S(2)}) collective-permute-start(f32[1,8,1024]{2,1,0:T(8,128)S(1)} %get-tuple-element.82), channel_id=1, source_target_pairs={{16,0},{32,16},{48,32},{64,48},{80,64},{96,80},{112,96},{17,1},{33... | collective-permute-start | bytes 98312 | tf_op jit(solution)/shard_map/ppermute | solution.py:23
  198.6 6.1 %collective-permute-start.17 = (f32[1,8,1024]{2,1,0:T(8,128)S(1)}, f32[1,8,1024]{2,1,0:T(8,128)S(1)}, u32[]{:S(2)}, u32[]{:S(2)}) collective-permute-start(f32[1,8,1024]{2,1,0:T(8,128)S(1)} %get-tuple-element.81), channel_id=1, source_target_pairs={{0,16},{16,32},{32,48},{48,64},{64,80},{80,96},{96,112},{1,17},{17... | collective-permute-start | bytes 98312 | tf_op jit(solution)/shard_map/ppermute | solution.py:22
  204.7 6.0 %collective-permute-start.18 = (f32[10,1,1024]{2,1,0:T(1,128)S(1)}, f32[10,1,1024]{2,1,0:T(1,128)S(1)}, u32[]{:S(2)}, u32[]{:S(2)}) collective-permute-start(f32[10,1,1024]{2,1,0:T(1,128)S(1)} %get-tuple-element.56), channel_id=1, source_target_pairs={{1,0},{2,1},{3,2},{4,3},{5,4},{6,5},{7,6},{8,7},{9,8},{10,9},{11,1... | collective-permute-start | bytes 122888 | tf_op jit(solution)/shard_map/ppermute | solution.py:23
  213.6 7.0 %collective-permute-start.20 = (f32[1,8,1024]{2,1,0:T(8,128)S(1)}, f32[1,8,1024]{2,1,0:T(8,128)S(1)}, u32[]{:S(2)}, u32[]{:S(2)}) collective-permute-start(f32[1,8,1024]{2,1,0:T(8,128)S(1)} %get-tuple-element.80), channel_id=1, source_target_pairs={{16,0},{32,16},{48,32},{64,48},{80,64},{96,80},{112,96},{17,1},{33... | collective-permute-start | bytes 98312 | tf_op jit(solution)/shard_map/ppermute | solution.py:23
  215.5 6.1 %collective-permute-start.21 = (f32[1,8,1024]{2,1,0:T(8,128)S(1)}, f32[1,8,1024]{2,1,0:T(8,128)S(1)}, u32[]{:S(2)}, u32[]{:S(2)}) collective-permute-start(f32[1,8,1024]{2,1,0:T(8,128)S(1)} %get-tuple-element.79), channel_id=1, source_target_pairs={{0,16},{16,32},{32,48},{48,64},{64,80},{80,96},{96,112},{1,17},{17... | collective-permute-start | bytes 98312 | tf_op jit(solution)/shard_map/ppermute | solution.py:22
  221.7 6.0 %collective-permute-start.22 = (f32[10,1,1024]{2,1,0:T(1,128)S(1)}, f32[10,1,1024]{2,1,0:T(1,128)S(1)}, u32[]{:S(2)}, u32[]{:S(2)}) collective-permute-start(f32[10,1,1024]{2,1,0:T(1,128)S(1)} %get-tuple-element.54), channel_id=1, source_target_pairs={{1,0},{2,1},{3,2},{4,3},{5,4},{6,5},{7,6},{8,7},{9,8},{10,9},{11,1... | collective-permute-start | bytes 122888 | tf_op jit(solution)/shard_map/ppermute | solution.py:23
  231.2 7.0 %collective-permute-start.24 = (f32[1,8,1024]{2,1,0:T(8,128)S(1)}, f32[1,8,1024]{2,1,0:T(8,128)S(1)}, u32[]{:S(2)}, u32[]{:S(2)}) collective-permute-start(f32[1,8,1024]{2,1,0:T(8,128)S(1)} %get-tuple-element.78), channel_id=1, source_target_pairs={{16,0},{32,16},{48,32},{64,48},{80,64},{96,80},{112,96},{17,1},{33... | collective-permute-start | bytes 98312 | tf_op jit(solution)/shard_map/ppermute | solution.py:23
  233.1 6.1 %collective-permute-start.25 = (f32[1,8,1024]{2,1,0:T(8,128)S(1)}, f32[1,8,1024]{2,1,0:T(8,128)S(1)}, u32[]{:S(2)}, u32[]{:S(2)}) collective-permute-start(f32[1,8,1024]{2,1,0:T(8,128)S(1)} %get-tuple-element.77), channel_id=1, source_target_pairs={{0,16},{16,32},{32,48},{48,64},{64,80},{80,96},{96,112},{1,17},{17... | collective-permute-start | bytes 98312 | tf_op jit(solution)/shard_map/ppermute | solution.py:22
  239.3 6.2 %collective-permute-start.26 = (f32[10,1,1024]{2,1,0:T(1,128)S(1)}, f32[10,1,1024]{2,1,0:T(1,128)S(1)}, u32[]{:S(2)}, u32[]{:S(2)}) collective-permute-start(f32[10,1,1024]{2,1,0:T(1,128)S(1)} %get-tuple-element.52), channel_id=1, source_target_pairs={{1,0},{2,1},{3,2},{4,3},{5,4},{6,5},{7,6},{8,7},{9,8},{10,9},{11,1... | collective-permute-start | bytes 122888 | tf_op jit(solution)/shard_map/ppermute | solution.py:23
  248.9 7.0 %collective-permute-start.28 = (f32[1,8,1024]{2,1,0:T(8,128)S(1)}, f32[1,8,1024]{2,1,0:T(8,128)S(1)}, u32[]{:S(2)}, u32[]{:S(2)}) collective-permute-start(f32[1,8,1024]{2,1,0:T(8,128)S(1)} %get-tuple-element.76), channel_id=1, source_target_pairs={{16,0},{32,16},{48,32},{64,48},{80,64},{96,80},{112,96},{17,1},{33... | collective-permute-start | bytes 98312 | tf_op jit(solution)/shard_map/ppermute | solution.py:23
  250.8 6.1 %collective-permute-start.29 = (f32[1,8,1024]{2,1,0:T(8,128)S(1)}, f32[1,8,1024]{2,1,0:T(8,128)S(1)}, u32[]{:S(2)}, u32[]{:S(2)}) collective-permute-start(f32[1,8,1024]{2,1,0:T(8,128)S(1)} %get-tuple-element.75), channel_id=1, source_target_pairs={{0,16},{16,32},{32,48},{48,64},{64,80},{80,96},{96,112},{1,17},{17... | collective-permute-start | bytes 98312 | tf_op jit(solution)/shard_map/ppermute | solution.py:22
  256.9 8.5 %collective-permute-start.30 = (f32[10,1,1024]{2,1,0:T(1,128)S(1)}, f32[10,1,1024]{2,1,0:T(1,128)S(1)}, u32[]{:S(2)}, u32[]{:S(2)}) collective-permute-start(f32[10,1,1024]{2,1,0:T(1,128)S(1)} %get-tuple-element.50), channel_id=1, source_target_pairs={{1,0},{2,1},{3,2},{4,3},{5,4},{6,5},{7,6},{8,7},{9,8},{10,9},{11,1... | collective-permute-start | bytes 122888 | tf_op jit(solution)/shard_map/ppermute | solution.py:23
  258.2 7.8 %collective-permute-start.31 = (f32[10,1,1024]{2,1,0:T(1,128)S(1)}, f32[10,1,1024]{2,1,0:T(1,128)S(1)}, u32[]{:S(2)}, u32[]{:S(2)}) collective-permute-start(f32[10,1,1024]{2,1,0:T(1,128)S(1)} %get-tuple-element.49), channel_id=1, source_target_pairs={{0,1},{1,2},{2,3},{3,4},{4,5},{5,6},{6,7},{7,8},{8,9},{9,10},{10,1... | collective-permute-start | bytes 122888 | tf_op jit(solution)/shard_map/ppermute | solution.py:22
  266.9 7.0 %collective-permute-start.32 = (f32[1,8,1024]{2,1,0:T(8,128)S(1)}, f32[1,8,1024]{2,1,0:T(8,128)S(1)}, u32[]{:S(2)}, u32[]{:S(2)}) collective-permute-start(f32[1,8,1024]{2,1,0:T(8,128)S(1)} %get-tuple-element.74), channel_id=1, source_target_pairs={{16,0},{32,16},{48,32},{64,48},{80,64},{96,80},{112,96},{17,1},{33... | collective-permute-start | bytes 98312 | tf_op jit(solution)/shard_map/ppermute | solution.py:23
  268.8 6.1 %collective-permute-start.33 = (f32[1,8,1024]{2,1,0:T(8,128)S(1)}, f32[1,8,1024]{2,1,0:T(8,128)S(1)}, u32[]{:S(2)}, u32[]{:S(2)}) collective-permute-start(f32[1,8,1024]{2,1,0:T(8,128)S(1)} %get-tuple-element.73), channel_id=1, source_target_pairs={{0,16},{16,32},{32,48},{48,64},{64,80},{80,96},{96,112},{1,17},{17... | collective-permute-start | bytes 98312 | tf_op jit(solution)/shard_map/ppermute | solution.py:22
  275.0 8.0 %collective-permute-start.34 = (f32[10,1,1024]{2,1,0:T(1,128)S(1)}, f32[10,1,1024]{2,1,0:T(1,128)S(1)}, u32[]{:S(2)}, u32[]{:S(2)}) collective-permute-start(f32[10,1,1024]{2,1,0:T(1,128)S(1)} %get-tuple-element.48), channel_id=1, source_target_pairs={{1,0},{2,1},{3,2},{4,3},{5,4},{6,5},{7,6},{8,7},{9,8},{10,9},{11,1... | collective-permute-start | bytes 122888 | tf_op jit(solution)/shard_map/ppermute | solution.py:23
  276.3 7.8 %collective-permute-start.35 = (f32[10,1,1024]{2,1,0:T(1,128)S(1)}, f32[10,1,1024]{2,1,0:T(1,128)S(1)}, u32[]{:S(2)}, u32[]{:S(2)}) collective-permute-start(f32[10,1,1024]{2,1,0:T(1,128)S(1)} %get-tuple-element.47), channel_id=1, source_target_pairs={{0,1},{1,2},{2,3},{3,4},{4,5},{5,6},{6,7},{7,8},{8,9},{9,10},{10,1... | collective-permute-start | bytes 122888 | tf_op jit(solution)/shard_map/ppermute | solution.py:22
  285.0 7.0 %collective-permute-start.36 = (f32[1,8,1024]{2,1,0:T(8,128)S(1)}, f32[1,8,1024]{2,1,0:T(8,128)S(1)}, u32[]{:S(2)}, u32[]{:S(2)}) collective-permute-start(f32[1,8,1024]{2,1,0:T(8,128)S(1)} %get-tuple-element.72), channel_id=1, source_target_pairs={{16,0},{32,16},{48,32},{64,48},{80,64},{96,80},{112,96},{17,1},{33... | collective-permute-start | bytes 98312 | tf_op jit(solution)/shard_map/ppermute | solution.py:23
  286.9 6.1 %collective-permute-start.37 = (f32[1,8,1024]{2,1,0:T(8,128)S(1)}, f32[1,8,1024]{2,1,0:T(8,128)S(1)}, u32[]{:S(2)}, u32[]{:S(2)}) collective-permute-start(f32[1,8,1024]{2,1,0:T(8,128)S(1)} %get-tuple-element.71), channel_id=1, source_target_pairs={{0,16},{16,32},{32,48},{48,64},{64,80},{80,96},{96,112},{1,17},{17... | collective-permute-start | bytes 98312 | tf_op jit(solution)/shard_map/ppermute | solution.py:22
  293.0 8.0 %collective-permute-start.38 = (f32[10,1,1024]{2,1,0:T(1,128)S(1)}, f32[10,1,1024]{2,1,0:T(1,128)S(1)}, u32[]{:S(2)}, u32[]{:S(2)}) collective-permute-start(f32[10,1,1024]{2,1,0:T(1,128)S(1)} %get-tuple-element.46), channel_id=1, source_target_pairs={{1,0},{2,1},{3,2},{4,3},{5,4},{6,5},{7,6},{8,7},{9,8},{10,9},{11,1... | collective-permute-start | bytes 122888 | tf_op jit(solution)/shard_map/ppermute | solution.py:23
  294.3 7.8 %collective-permute-start.39 = (f32[10,1,1024]{2,1,0:T(1,128)S(1)}, f32[10,1,1024]{2,1,0:T(1,128)S(1)}, u32[]{:S(2)}, u32[]{:S(2)}) collective-permute-start(f32[10,1,1024]{2,1,0:T(1,128)S(1)} %get-tuple-element.45), channel_id=1, source_target_pairs={{0,1},{1,2},{2,3},{3,4},{4,5},{5,6},{6,7},{7,8},{8,9},{9,10},{10,1... | collective-permute-start | bytes 122888 | tf_op jit(solution)/shard_map/ppermute | solution.py:22
  304.4 7.9 %collective-permute-start.40 = (f32[1,8,1024]{2,1,0:T(8,128)}, f32[1,8,1024]{2,1,0:T(8,128)}, u32[]{:S(2)}, u32[]{:S(2)}) collective-permute-start(f32[1,8,1024]{2,1,0:T(8,128)} %get-tuple-element.70), channel_id=1, source_target_pairs={{16,0},{32,16},{48,32},{64,48},{80,64},{96,80},{112,96},{17,1},{33... | collective-permute-start | bytes 98312 | tf_op jit(solution)/shard_map/ppermute | solution.py:23
  306.3 6.4 %collective-permute-start.41 = (f32[1,8,1024]{2,1,0:T(8,128)}, f32[1,8,1024]{2,1,0:T(8,128)}, u32[]{:S(2)}, u32[]{:S(2)}) collective-permute-start(f32[1,8,1024]{2,1,0:T(8,128)} %get-tuple-element.69), channel_id=1, source_target_pairs={{0,16},{16,32},{32,48},{48,64},{64,80},{80,96},{96,112},{1,17},{17... | collective-permute-start | bytes 98312 | tf_op jit(solution)/shard_map/ppermute | solution.py:22
  313.6 8.1 %collective-permute-start.42 = (f32[10,1,1024]{2,1,0:T(1,128)S(1)}, f32[10,1,1024]{2,1,0:T(1,128)S(1)}, u32[]{:S(2)}, u32[]{:S(2)}) collective-permute-start(f32[10,1,1024]{2,1,0:T(1,128)S(1)} %get-tuple-element.44), channel_id=1, source_target_pairs={{1,0},{2,1},{3,2},{4,3},{5,4},{6,5},{7,6},{8,7},{9,8},{10,9},{11,1... | collective-permute-start | bytes 122888 | tf_op jit(solution)/shard_map/ppermute | solution.py:23
  314.9 7.8 %collective-permute-start.43 = (f32[10,1,1024]{2,1,0:T(1,128)S(1)}, f32[10,1,1024]{2,1,0:T(1,128)S(1)}, u32[]{:S(2)}, u32[]{:S(2)}) collective-permute-start(f32[10,1,1024]{2,1,0:T(1,128)S(1)} %get-tuple-element.43), channel_id=1, source_target_pairs={{0,1},{1,2},{2,3},{3,4},{4,5},{5,6},{6,7},{7,8},{8,9},{9,10},{10,1... | collective-permute-start | bytes 122888 | tf_op jit(solution)/shard_map/ppermute | solution.py:22
  325.4 7.0 %collective-permute-start.44 = (f32[1,8,1024]{2,1,0:T(8,128)S(1)}, f32[1,8,1024]{2,1,0:T(8,128)S(1)}, u32[]{:S(2)}, u32[]{:S(2)}) collective-permute-start(f32[1,8,1024]{2,1,0:T(8,128)S(1)} %get-tuple-element.68), channel_id=1, source_target_pairs={{16,0},{32,16},{48,32},{64,48},{80,64},{96,80},{112,96},{17,1},{33... | collective-permute-start | bytes 98312 | tf_op jit(solution)/shard_map/ppermute | solution.py:23
  327.4 6.1 %collective-permute-start.45 = (f32[1,8,1024]{2,1,0:T(8,128)S(1)}, f32[1,8,1024]{2,1,0:T(8,128)S(1)}, u32[]{:S(2)}, u32[]{:S(2)}) collective-permute-start(f32[1,8,1024]{2,1,0:T(8,128)S(1)} %get-tuple-element.67), channel_id=1, source_target_pairs={{0,16},{16,32},{32,48},{48,64},{64,80},{80,96},{96,112},{1,17},{17... | collective-permute-start | bytes 98312 | tf_op jit(solution)/shard_map/ppermute | solution.py:22
  333.5 8.0 %collective-permute-start.46 = (f32[10,1,1024]{2,1,0:T(1,128)S(1)}, f32[10,1,1024]{2,1,0:T(1,128)S(1)}, u32[]{:S(2)}, u32[]{:S(2)}) collective-permute-start(f32[10,1,1024]{2,1,0:T(1,128)S(1)} %get-tuple-element.42), channel_id=1, source_target_pairs={{1,0},{2,1},{3,2},{4,3},{5,4},{6,5},{7,6},{8,7},{9,8},{10,9},{11,1... | collective-permute-start | bytes 122888 | tf_op jit(solution)/shard_map/ppermute | solution.py:23
  334.8 7.8 %collective-permute-start.47 = (f32[10,1,1024]{2,1,0:T(1,128)S(1)}, f32[10,1,1024]{2,1,0:T(1,128)S(1)}, u32[]{:S(2)}, u32[]{:S(2)}) collective-permute-start(f32[10,1,1024]{2,1,0:T(1,128)S(1)} %get-tuple-element.41), channel_id=1, source_target_pairs={{0,1},{1,2},{2,3},{3,4},{4,5},{5,6},{6,7},{7,8},{8,9},{9,10},{10,1... | collective-permute-start | bytes 122888 | tf_op jit(solution)/shard_map/ppermute | solution.py:22
  343.7 7.1 %collective-permute-start.48 = (f32[1,8,1024]{2,1,0:T(8,128)S(1)}, f32[1,8,1024]{2,1,0:T(8,128)S(1)}, u32[]{:S(2)}, u32[]{:S(2)}) collective-permute-start(f32[1,8,1024]{2,1,0:T(8,128)S(1)} %get-tuple-element.66), channel_id=1, source_target_pairs={{16,0},{32,16},{48,32},{64,48},{80,64},{96,80},{112,96},{17,1},{33... | collective-permute-start | bytes 98312 | tf_op jit(solution)/shard_map/ppermute | solution.py:23
  345.6 6.1 %collective-permute-start.49 = (f32[1,8,1024]{2,1,0:T(8,128)S(1)}, f32[1,8,1024]{2,1,0:T(8,128)S(1)}, u32[]{:S(2)}, u32[]{:S(2)}) collective-permute-start(f32[1,8,1024]{2,1,0:T(8,128)S(1)} %get-tuple-element.65), channel_id=1, source_target_pairs={{0,16},{16,32},{32,48},{48,64},{64,80},{80,96},{96,112},{1,17},{17... | collective-permute-start | bytes 98312 | tf_op jit(solution)/shard_map/ppermute | solution.py:22
  351.7 8.7 %collective-permute-start.50 = (f32[10,1,1024]{2,1,0:T(1,128)S(1)}, f32[10,1,1024]{2,1,0:T(1,128)S(1)}, u32[]{:S(2)}, u32[]{:S(2)}) collective-permute-start(f32[10,1,1024]{2,1,0:T(1,128)S(1)} %get-tuple-element.40), channel_id=1, source_target_pairs={{1,0},{2,1},{3,2},{4,3},{5,4},{6,5},{7,6},{8,7},{9,8},{10,9},{11,1... | collective-permute-start | bytes 122888 | tf_op jit(solution)/shard_map/ppermute | solution.py:23
  353.0 7.8 %collective-permute-start.51 = (f32[10,1,1024]{2,1,0:T(1,128)S(1)}, f32[10,1,1024]{2,1,0:T(1,128)S(1)}, u32[]{:S(2)}, u32[]{:S(2)}) collective-permute-start(f32[10,1,1024]{2,1,0:T(1,128)S(1)} %get-tuple-element.39), channel_id=1, source_target_pairs={{0,1},{1,2},{2,3},{3,4},{4,5},{5,6},{6,7},{7,8},{8,9},{9,10},{10,1... | collective-permute-start | bytes 122888 | tf_op jit(solution)/shard_map/ppermute | solution.py:22
  468.2 44.9 %all-to-all-start = ((f32[16,1,32768]{2,1,0:T(1,128)}), f32[16,1,32768]{2,1,0:T(1,128)}, u32[]{:S(2)}, u32[]{:S(2)}) async-start(f32[16,1,32768]{2,1,0:T(1,128)} %reshape.173), calls=%async_computation | async-start | bytes 4194304 | tf_op jit(solution)/shard_map/all_to_all | solution.py:131
  579.7 9.6 %collective-permute-start.55 = (f32[4,8,128]{2,1,0:T(8,128)S(1)}, f32[4,8,128]{2,1,0:T(8,128)S(1)}, u32[]{:S(2)}, u32[]{:S(2)}) collective-permute-start(f32[4,8,128]{2,1,0:T(8,128)S(1)} %get-tuple-element.7), channel_id=1, source_target_pairs={{0,1},{1,2},{2,3},{3,4},{4,5},{5,6},{6,7},{7,8},{8,9},{9,10},{10,1... | collective-permute-start | bytes 49160 | tf_op jit(solution)/shard_map/ppermute | solution.py:31
  581.9 11.3 %collective-permute-start.52 = (f32[4,1,128,128]{3,2,1,0:T(8,128)S(1)}, f32[4,1,128,128]{3,2,1,0:T(8,128)S(1)}, u32[]{:S(2)}, u32[]{:S(2)}) collective-permute-start(f32[4,1,128,128]{3,2,1,0:T(8,128)S(1)} %get-tuple-element.35), channel_id=1, source_target_pairs={{16,0},{32,16},{48,32},{64,48},{80,64},{96,80},{112,96},{17,1},{33... | collective-permute-start | bytes 786440 | tf_op jit(solution)/shard_map/ppermute | solution.py:23
  583.9 9.3 %collective-permute-start.53 = (f32[4,1,128,128]{3,2,1,0:T(8,128)S(1)}, f32[4,1,128,128]{3,2,1,0:T(8,128)S(1)}, u32[]{:S(2)}, u32[]{:S(2)}) collective-permute-start(f32[4,1,128,128]{3,2,1,0:T(8,128)S(1)} %get-tuple-element.36), channel_id=1, source_target_pairs={{0,16},{16,32},{32,48},{48,64},{64,80},{80,96},{96,112},{1,17},{17... | collective-permute-start | bytes 786440 | tf_op jit(solution)/shard_map/ppermute | solution.py:22
  (40 other events, 558.6 us)
where the time goes:
time: 608 us; the launch traced here: 596 us
  starting transfers between devices  201 us (33%)
  local copies, waits for them, and re-layouts  139 us (23%)
  blocking collectives  134 us (22%)
  other arithmetic  70.3 us (12%)
  waiting for transfers between devices  44.9 us (7%)
  between operations  6.58 us (1%)
    ppermute x27, starting transfers between devices, extended(): before = lax.ppermute(last, axis, up)  137 us
    pmax x1, blocking collectives, local(): high = lax.pmax(upper_local, ('gx', 'yz'))  71 us
    pmin x1, blocking collectives, local(): low = lax.pmin(lower_local, ('gx', 'yz'))  63.2 us
    unnamed x68, local copies, waits for them, and re-layouts  59.3 us
    ppermute x27, starting transfers between devices, extended(): after = lax.ppermute(initial, axis, down)  44.6 us
    gather x1, local copies, waits for them, and re-layouts, local(): sent = jnp.take(padded_field, where_from, axis=3) * valid  32.7 us
    unnamed x1, other arithmetic  26.9 us
    all_to_all x1, waiting for transfers between devices, local(): lax.all_to_all(sent, 'yz', split_axis=3, concat_axis=2, tiled=True)  23.7 us
  transfers between devices with their start and end apart: 57, of which 23 were waited for; matrix products, arithmetic and copies ran while one was open for 2% of the time, Pallas kernels for 0%

commit v1 on v0

v1 whole, which is shorter than its diff:
```python
import functools

import jax
import jax.numpy as jnp
from jax import lax
from jax.experimental import pallas as pl
from jax.experimental.pallas import tpu as pltpu
from jax.sharding import PartitionSpec as P

NCHEB = 6
ZMAX = 128
NG, NY = 8, 16
B = 8
H = 6
N = B + 2 * H
LO, HI = H, H + B
KT = 8
LEVELS = NCHEB - 1
MESH = pl.DeviceIdType.MESH
F32 = jnp.float32


def corner_rects(width):
    if width == 6:
        return [(1, 2, 5), (3, 5, 3)]
    if width == 5:
        return [(1, 2, 4), (3, 4, 2)]
    return []


def kernel(
    x0_hbm, k_hbm, c_hbm, f_hbm, u_hbm, lab, table, tally,
    t_out, r_out,
    nat, natu, kb, cb, xb, fb, v0, v1, e, rb, fx, fy, fz, db,
    ust, uest, u, ue, tst, test, t, te, natt, ytr,
    mu, beta, ar1, ar2, arst, coefs, starts,
    lsem, lusem, hs, hr, a1s, a1r, a2s, a2r, us, ur, ues, uer, ts, tr, tes, ter, ps, pr, osem,
):
    g, y = lax.axis_index("gx"), lax.axis_index("yz")
    gp, gm = lax.rem(g + 1, NG), lax.rem(g + NG - 1, NG)
    yp, ym = lax.rem(y + 1, NY), lax.rem(y + NY - 1, NY)
    along_y = [(g, lax.rem(y + k, NY)) for k in range(1, NY)]
    along_g = [(lax.rem(g + k, NG), y) for k in range(1, NG)]
    diagonal = [(gp, yp), (gm, ym), (gp, ym), (gm, yp)]

    fields = [k_hbm, x0_hbm, c_hbm, f_hbm]
    own_in = [
        [
            pltpu.make_async_copy(
                field.at[:, :, pl.ds(kt * 128, 128)], nat.at[n, :, pl.ds(kt * 8, 8)], lsem.at[n, kt]
            )
            for kt in range(KT)
        ]
        for n, field in enumerate(fields)
    ]
    u_in = [
        pltpu.make_async_copy(
            u_hbm.at[:, :, :, pl.ds(kt * 128, 128)], natu.at[:, :, kt + 1], lusem.at[kt]
        )
        for kt in range(KT)
    ]
    for copies in own_in:
        for copy in copies:
            copy.start()
    for copy in u_in:
        copy.start()

    barrier = pltpu.get_barrier_semaphore()
    for peer in along_y + along_g + diagonal:
        pl.semaphore_signal(barrier, inc=1, device_id=peer, device_id_type=MESH)

    zero_tile = jnp.zeros((8, 128), F32)
    for a in range(3):
        def zero_u(i, _, a=a):
            u[a, i, pl.ds(0, 8)] = zero_tile
            u[a, i, pl.ds(8 + 128, 8)] = zero_tile
            return 0
        lax.fori_loop(0, B + 2, zero_u, 0)

        def zero_natu(i, _, a=a):
            natu[a, i, 0] = zero_tile
            natu[a, i, KT + 1] = zero_tile
            return 0
        lax.fori_loop(0, B, zero_natu, 0)

    def zero_t(i, _):
        t[i, pl.ds(0, 8)] = zero_tile
        t[i, pl.ds(8 + 128, 8)] = zero_tile
        return 0
    lax.fori_loop(0, B + 2, zero_t, 0)

    def zero_natt(i, _):
        natt[i, 0] = zero_tile
        natt[i, KT + 1] = zero_tile
        return 0
    lax.fori_loop(0, B, zero_natt, 0)

    def to_lines(n, dst):
        def row(i, _):
            for j in range(B):
                dst[LO + i, LO + j] = nat[n, i, pl.ds(j, 8, stride=8), :]
            return 0
        lax.fori_loop(0, B, row, 0)

    for n, dst in ((0, kb), (1, xb), (2, cb), (3, fb)):
        for copy in own_in[n]:
            copy.wait()
        to_lines(n, dst)

    pl.semaphore_wait(barrier, len(along_y) + len(along_g) + len(diagonal))

    def halo(buf, width, slot):
        own, low, high = pl.ds(LO, B), pl.ds(LO - width, width), pl.ds(HI, width)
        first, last = pl.ds(LO, width), pl.ds(HI - width, width)
        moves = [
            (buf.at[own, last], buf.at[own, low], (g, yp)),
            (buf.at[own, first], buf.at[own, high], (g, ym)),
            (buf.at[last, own], buf.at[low, own], (gp, y)),
            (buf.at[first, own], buf.at[high, own], (gm, y)),
        ]
        for a0, a1, b1 in corner_rects(width):
            rows = a1 - a0 + 1
            li, lj = LO - a1, LO - b1
            hi, hj = HI - 1 + a0, HI
            for peer, i, j, si, sj in (
                ((gp, yp), li, lj, B, B),
                ((gm, ym), hi, hj, -B, -B),
                ((gp, ym), li, hj, B, -B),
                ((gm, yp), hi, lj, -B, B),
            ):
                moves.append(
                    (
                        buf.at[pl.ds(i + si, rows), pl.ds(j + sj, b1)],
                        buf.at[pl.ds(i, rows), pl.ds(j, b1)],
                        peer,
                    )
                )
        return [
            pltpu.make_async_remote_copy(
                src_ref=src, dst_ref=dst, send_sem=hs.at[slot, m], recv_sem=hr.at[slot, m],
                device_id=peer, device_id_type=MESH,
            )
            for m, (src, dst, peer) in enumerate(moves)
        ]

    x0_moves, k_moves, c_moves = halo(xb, 1, 0), halo(kb, 6, 1), halo(cb, 5, 2)
    for copy in x0_moves + k_moves + c_moves:
        copy.start()

    total = jnp.int32(0)
    for p in range(NY):
        starts[p] = total
        total = total + tally[p]

    eye = lax.broadcasted_iota(jnp.int32, (128, 128), 0) == lax.broadcasted_iota(jnp.int32, (128, 128), 1)

    def column_row(i, _):
        row = jnp.broadcast_to(lab[pl.ds(i, 1), :].astype(F32), (128, 128))
        column = jnp.sum(jnp.where(eye, row, 0.0), axis=1, keepdims=True)
        label = jnp.broadcast_to(column, (128, 128))
        for dst, r in ((mu, 0), (beta, 1)):
            dst[i] = jnp.where(label == 0.0, table[r, 0], 0.0) + jnp.where(label == 1.0, table[r, 1], 0.0)
        return 0
    lax.fori_loop(0, B, column_row, 0)

    lane = lax.broadcasted_iota(jnp.int32, (8, 128), 1)

    def pack(line, p, lane_of):
        start = starts[p]
        tile, off = start >> 7, start & 127
        window = jnp.where(lane >= off, line[tile + 1], line[tile + 2])
        before = start - 1 + 128
        after = start + tally[p] + 128
        prev = pltpu.roll(line[before >> 7], (lane_of - (before & 127) + 256) & 127, 1)
        nxt = pltpu.roll(line[after >> 7], (32 + lane_of - (after & 127) + 256) & 127, 1)
        return pltpu.roll(window, (128 - off) & 127, 1), prev, nxt

    for copy in u_in:
        copy.wait()

    def pack_u(p, _):
        edge = zero_tile
        for a in range(3):
            def one(i, edge, a=a):
                at = a * 8 + i
                window, prev, nxt = pack(natu.at[a, i], p, at)
                ust[p, a, i] = window
                return jnp.where(lane == at, prev, jnp.where(lane == at + 32, nxt, edge))
            edge = lax.fori_loop(0, B, one, edge)
        uest[p] = edge
        return 0
    lax.fori_loop(0, NY, pack_u, 0)

    def iota(n, axis):
        return lax.broadcasted_iota(jnp.int32, (n, 8, 128), axis)

    def up(v):
        by_lane = pltpu.roll(v, 127, 2)
        return jnp.where(iota(v.shape[0], 2) == 127, pltpu.roll(by_lane, 7, 1), by_lane)

    def down(v):
        by_lane = pltpu.roll(v, 1, 2)
        return jnp.where(iota(v.shape[0], 2) == 0, pltpu.roll(by_lane, 1, 1), by_lane)

    def harmonic(first, second):
        return 2.0 * first * second / (first + second)

    inside_low_g = jnp.where(g > 0, 1.0, 0.0)
    inside_high_g = jnp.where(g < NG - 1, 1.0, 0.0)
    inside_low_y = jnp.where(y > 0, 1.0, 0.0)
    inside_high_y = jnp.where(y < NY - 1, 1.0, 0.0)

    def faces(q):
        lo, n = LO - q, B + 2 * q
        half = n // 2
        chunks = [(lo, half), (lo + half, n - half)]

        def fx_row(i, _):
            for j0, c in chunks:
                at = pl.ds(j0, c)
                fx[i, at] = harmonic(kb[i, at], kb[i + 1, at])
            return 0
        lax.fori_loop(lo - 1, lo + n, fx_row, 0)

        fx[LO - 1, pl.ds(lo, n)] = fx[LO - 1, pl.ds(lo, n)] * inside_low_g
        fx[HI - 1, pl.ds(lo, n)] = fx[HI - 1, pl.ds(lo, n)] * inside_high_g

        def row(i, _):
            fy[i, lo - 1] = harmonic(kb[i, lo - 1], kb[i, lo])
            for j0, c in chunks:
                at = pl.ds(j0, c)
                own = kb[i, at]
                fy[i, at] = harmonic(own, kb[i, pl.ds(j0 + 1, c)])
                last = (iota(c, 1) == 7) & (iota(c, 2) == 127)
                fz[i, at] = jnp.where(last, 0.0, harmonic(own, up(own)))
            fy[i, LO - 1] = fy[i, LO - 1] * inside_low_y
            fy[i, HI - 1] = fy[i, HI - 1] * inside_high_y
            for j0, c in chunks:
                at = pl.ds(j0, c)
                z = fz[i, at]
                db[i, at] = (
                    cb[i, at] + fx[i, at] + fx[i - 1, at] + fy[i, at] + fy[i, pl.ds(j0 - 1, c)] + z + down(z)
                )
            return 0
        lax.fori_loop(lo, lo + n, row, 0)

    def applied(v, i, j0, c):
        at = pl.ds(j0, c)
        own, z = v[i, at], fz[i, at]
        return (
            db[i, at] * own
            - fx[i, at] * v[i + 1, at]
            - fx[i - 1, at] * v[i - 1, at]
            - fy[i, at] * v[i, pl.ds(j0 + 1, c)]
            - fy[i, pl.ds(j0 - 1, c)] * v[i, pl.ds(j0 - 1, c)]
            - z * up(own)
            - down(z * own)
        )

    def first_residual(x, dst):
        def row(i, _):
            at = pl.ds(LO, B)
            dst[i, at] = fb[i, at] + (cb[i, at] * x[i, at] - applied(x, i, LO, B))
            return 0
        lax.fori_loop(LO, HI, row, 0)

    for copy in x0_moves + k_moves[:4]:
        copy.wait_recv()
    faces(0)

    def bound_row(i, carry):
        most, least = carry
        at = pl.ds(LO, B)
        c = cb[i, at]
        return (
            jnp.maximum(most, jnp.max(2.0 * db[i, at] - c, axis=0)),
            jnp.maximum(least, jnp.max(-c, axis=0)),
        )
    neg = jnp.full((8, 128), -3.0e38, F32)
    most, least = lax.fori_loop(LO, HI, bound_row, (neg, neg))
    sub = lax.broadcasted_iota(jnp.int32, (8, 128), 0)

    def over_rows(v):
        return jnp.broadcast_to(jnp.max(v, axis=0, keepdims=True), (8, 128))

    arst[0] = jnp.where(sub < 4, over_rows(most), over_rows(least))
    ar1[y] = arst[0]
    ar1_moves = [
        pltpu.make_async_remote_copy(
            src_ref=arst.at[0], dst_ref=ar1.at[y], send_sem=a1s.at[k], recv_sem=a1r.at[k],
            device_id=peer, device_id_type=MESH,
        )
        for k, peer in enumerate(along_y)
    ]
    for copy in ar1_moves:
        copy.start()

    first_residual(xb, v0)
    v0_moves = halo(v0, 6, 3)
    for copy in v0_moves:
        copy.start()

    rows_of_me = pl.ds(pl.multiple_of(8 + 8 * y, 8), 8)

    def u_copies(k):
        p = lax.rem(y + k, NY)
        peer = (g, p)
        return [
            pltpu.make_async_remote_copy(
                src_ref=ust.at[p], dst_ref=u.at[:, pl.ds(1, B), rows_of_me],
                send_sem=us.at[k], recv_sem=ur.at[k], device_id=peer, device_id_type=MESH,
            ),
            pltpu.make_async_remote_copy(
                src_ref=uest.at[p], dst_ref=ue.at[rows_of_me],
                send_sem=ues.at[k], recv_sem=uer.at[k], device_id=peer, device_id_type=MESH,
            ),
        ]

    u_moves = [u_copies(k) for k in range(1, NY)]
    u_own = [
        pltpu.make_async_copy(ust.at[y], u.at[:, pl.ds(1, B), rows_of_me], us.at[0]),
        pltpu.make_async_copy(uest.at[y], ue.at[rows_of_me], ues.at[0]),
    ]
    for copies in u_moves[:8]:
        for copy in copies:
            copy.start()
    for copy in u_own:
        copy.start()

    for copy in k_moves[4:] + c_moves:
        copy.wait_recv()
    faces(5)

    for copy in ar1_moves:
        copy.wait_recv()
    arst[1] = jnp.max(ar1[...], axis=0)
    ar2[g] = arst[1]
    ar2_moves = [
        pltpu.make_async_remote_copy(
            src_ref=arst.at[1], dst_ref=ar2.at[g], send_sem=a2s.at[k], recv_sem=a2r.at[k],
            device_id=peer, device_id_type=MESH,
        )
        for k, peer in enumerate(along_g)
    ]
    for copy in ar2_moves:
        copy.start()
    for copy in ar2_moves:
        copy.wait_recv()
    bounds = jnp.max(jnp.max(ar2[...], axis=0), axis=1, keepdims=True)
    high = jnp.broadcast_to(bounds[0:1], (8, 128))
    low = -jnp.broadcast_to(bounds[4:5], (8, 128))
    theta = (high + low) / 2.0
    delta = (high - low) / 2.0
    sigma = theta / delta
    rho = 1.0 / sigma
    coefs[0] = 1.0 / theta
    for turn in range(LEVELS):
        rho_new = 1.0 / (2.0 * sigma - rho)
        coefs[1 + 2 * turn] = rho_new * rho
        coefs[2 + 2 * turn] = 2.0 * rho_new / delta * theta
        rho = rho_new

    def level(src, turn, q):
        lo, n = LO - q, B + 2 * q
        parts = 2 if n > 8 else 1
        c = n // parts
        inv, alpha, bet = coefs[0], coefs[1 + 2 * turn], coefs[2 + 2 * turn]
        before = src if turn == 0 else rb

        def row(i, _):
            for part in range(parts):
                j0 = lo + part * c
                at = pl.ds(j0, c)
                resid = before[i, at] - inv[None] * applied(src, i, j0, c)
                rb[i, at] = resid
                e[turn, i, at] = alpha[None] * src[i, at] + bet[None] * resid
            return 0
        lax.fori_loop(lo, lo + n, row, 0)

    def heat_step(start, q):
        src = start
        for turn in range(LEVELS):
            level(src, turn, q - 1 - turn)
            src = e.at[turn]

    def summed(start, i, at):
        total = start[i, at]
        for turn in range(LEVELS):
            total = total + e[turn, i, at]
        return xb[i, at] + coefs[0][None] * total

    for copy in v0_moves:
        copy.wait_recv()
    heat_step(v0, 6)

    for copy in x0_moves:
        copy.wait_send()

    def next_x(i, _):
        at = pl.ds(LO - 1, B + 2)
        xb[i, at] = summed(v0, i, at)
        return 0
    lax.fori_loop(LO - 1, HI + 1, next_x, 0)

    first_residual(xb, v1)
    v1_moves = halo(v1, 5, 4)
    for copy in v1_moves:
        copy.start()
    for copies in u_moves[8:]:
        for copy in copies:
            copy.start()
    for copy in v1_moves:
        copy.wait_recv()
    heat_step(v1, 5)

    def last_x(i, _):
        final = summed(v1, LO + i, pl.ds(LO, B))
        for j in range(B):
            ytr[i, pl.ds(j * 8, 8)] = final[j]
        return 0
    lax.fori_loop(0, B, last_x, 0)

    def to_natural(i, _):
        for kt in range(KT):
            natt[i, kt + 1] = ytr[i, pl.ds(kt, 8, stride=8), :]
        return 0
    lax.fori_loop(0, B, to_natural, 0)

    t_copies_out = [
        pltpu.make_async_copy(natt.at[:, kt + 1], t_out.at[:, :, pl.ds(kt * 128, 128)], osem.at[kt])
        for kt in range(KT)
    ]
    for copy in t_copies_out:
        copy.start()

    def pack_t(p, _):
        def one(i, edge):
            window, prev, nxt = pack(natt.at[i], p, i)
            tst[p, i] = window
            return jnp.where(lane == i, prev, jnp.where(lane == i + 32, nxt, edge))
        test[p] = lax.fori_loop(0, B, one, zero_tile)
        return 0
    lax.fori_loop(0, NY, pack_t, 0)

    def t_copies(k):
        p = lax.rem(y + k, NY)
        peer = (g, p)
        return [
            pltpu.make_async_remote_copy(
                src_ref=tst.at[p], dst_ref=t.at[pl.ds(1, B), rows_of_me],
                send_sem=ts.at[k], recv_sem=tr.at[k], device_id=peer, device_id_type=MESH,
            ),
            pltpu.make_async_remote_copy(
                src_ref=test.at[p], dst_ref=te.at[rows_of_me],
                send_sem=tes.at[k], recv_sem=ter.at[k], device_id=peer, device_id_type=MESH,
            ),
        ]

    t_moves = [t_copies(k) for k in range(1, NY)]
    t_own = [
        pltpu.make_async_copy(tst.at[y], t.at[pl.ds(1, B), rows_of_me], ts.at[0]),
        pltpu.make_async_copy(test.at[y], te.at[rows_of_me], tes.at[0]),
    ]
    for copies in t_moves:
        for copy in copies:
            copy.start()
    for copy in t_own:
        copy.start()

    for copy in u_own:
        copy.wait()
    for copies in u_moves:
        for copy in copies:
            copy.wait_recv()
    inner = pl.ds(8, 128)

    def plane_copies(buf, at, slot):
        return [
            pltpu.make_async_remote_copy(
                src_ref=buf.at[at(B)], dst_ref=buf.at[at(0)],
                send_sem=ps.at[slot, 0], recv_sem=pr.at[slot, 0], device_id=(gp, y), device_id_type=MESH,
            ),
            pltpu.make_async_remote_copy(
                src_ref=buf.at[at(1)], dst_ref=buf.at[at(B + 1)],
                send_sem=ps.at[slot, 1], recv_sem=pr.at[slot, 1], device_id=(gm, y), device_id_type=MESH,
            ),
        ]

    u_planes = plane_copies(u, lambda i: (slice(None), i, inner), 0)
    for copy in u_planes:
        copy.start()

    length = tally[y]
    wide_lane = lax.broadcasted_iota(jnp.int32, (128, 128), 1)
    valid = wide_lane < length

    def beside(own, edges, at):
        nxt = pltpu.roll(edges, (length - 1 - 32 - at + 256) & 127, 1)
        prev = pltpu.roll(edges, (128 - at) & 127, 1)
        plus = jnp.where(wide_lane == length - 1, nxt, pltpu.roll(own, 127, 1))
        minus = jnp.where(wide_lane == 0, prev, pltpu.roll(own, 1, 1))
        return plus, minus

    for copy in u_planes:
        copy.wait_recv()
    for a in range(3):
        u[a, 0, inner] = u[a, 0, inner] * inside_low_g
        u[a, B + 1, inner] = u[a, B + 1, inner] * inside_high_g

        def disp_row(i, _, a=a):
            own = u[a, i + 1, inner]
            plus, minus = beside(own, ue[inner], a * 8 + i)
            total = (
                u[a, i + 2, inner] + u[a, i, inner] + u[a, i + 1, pl.ds(9, 128)] + u[a, i + 1, pl.ds(7, 128)]
                + plus + minus
            )
            r_out[a, i] = mu[i] * (6.0 * own - total)
            return 0
        lax.fori_loop(0, B, disp_row, 0)

    for copy in t_own:
        copy.wait()
    for copies in t_moves:
        for copy in copies:
            copy.wait_recv()

    def stress_row(i, _):
        t[i + 1, inner] = beta[i] * t[i + 1, inner]
        return 0
    lax.fori_loop(0, B, stress_row, 0)
    t_planes = plane_copies(t, lambda i: (i, inner), 1)
    for copy in t_planes:
        copy.start()

    def stress_jk(i, _):
        own = t[i + 1, inner]
        plus, minus = beside(own, beta[i] * te[inner], i)
        along_j = t[i + 1, pl.ds(9, 128)] - t[i + 1, pl.ds(7, 128)]
        r_out[1, i] = jnp.where(valid, r_out[1, i] + 0.5 * along_j, 0.0)
        r_out[2, i] = jnp.where(valid, r_out[2, i] + 0.5 * (plus - minus), 0.0)
        return 0
    lax.fori_loop(0, B, stress_jk, 0)

    for copy in t_planes:
        copy.wait_recv()
    t[0, inner] = t[0, inner] * inside_low_g
    t[B + 1, inner] = t[B + 1, inner] * inside_high_g

    def stress_i(i, _):
        r_out[0, i] = jnp.where(valid, r_out[0, i] + 0.5 * (t[i + 2, inner] - t[i, inner]), 0.0)
        return 0
    lax.fori_loop(0, B, stress_i, 0)

    for copy in k_moves + c_moves + v0_moves + v1_moves + ar1_moves + ar2_moves + u_planes + t_planes:
        copy.wait_send()
    for copies in u_moves + t_moves:
        for copy in copies:
            copy.wait_send()
    for copy in t_copies_out:
        copy.wait()


def local(
    starting_warmth_level,
    diffusive_coefficient_map,
    specific_warmth_store,
    energy_source_flux,
    deformation_vector,
    substance_label_columns,
    substance_moduli_table,
    subdomain_point_tally,
):
    hbm = pl.BlockSpec(memory_space=pl.ANY)
    vmem = pl.BlockSpec(memory_space=pltpu.VMEM)
    smem = pl.BlockSpec(memory_space=pltpu.SMEM)
    grid = pltpu.VMEM((N, N, 8, 128), F32)
    dma = pltpu.SemaphoreType.DMA
    return pl.pallas_call(
        kernel,
        out_shape=(
            jax.ShapeDtypeStruct((B, B, KT * 128), F32),
            jax.ShapeDtypeStruct((3, B, NY * 8, ZMAX), F32),
        ),
        in_specs=[hbm] * 5 + [vmem, smem, smem],
        out_specs=(hbm, vmem),
        scratch_shapes=[
            pltpu.VMEM((4, B, KT * 8, 128), F32),
            pltpu.VMEM((3, B, KT + 2, 8, 128), F32),
            grid, grid, grid, grid, grid, grid,
            pltpu.VMEM((LEVELS, N, N, 8, 128), F32),
            grid, grid, grid, grid, grid,
            pltpu.VMEM((NY, 3, B, 8, 128), F32),
            pltpu.VMEM((NY, 8, 128), F32),
            pltpu.VMEM((3, B + 2, 8 + 128 + 8, 128), F32),
            pltpu.VMEM((8 + 128 + 8, 128), F32),
            pltpu.VMEM((NY, B, 8, 128), F32),
            pltpu.VMEM((NY, 8, 128), F32),
            pltpu.VMEM((B + 2, 8 + 128 + 8, 128), F32),
            pltpu.VMEM((8 + 128 + 8, 128), F32),
            pltpu.VMEM((B, KT + 2, 8, 128), F32),
            pltpu.VMEM((B, B * 8, 128), F32),
            pltpu.VMEM((B, 128, 128), F32),
            pltpu.VMEM((B, 128, 128), F32),
            pltpu.VMEM((NY, 8, 128), F32),
            pltpu.VMEM((NG, 8, 128), F32),
            pltpu.VMEM((2, 8, 128), F32),
            pltpu.VMEM((1 + 2 * LEVELS, 8, 128), F32),
            pltpu.SMEM((NY,), jnp.int32),
            dma((4, KT)), dma((KT,)),
            dma((5, 12)), dma((5, 12)),
            dma((NY - 1,)), dma((NY - 1,)), dma((NG - 1,)), dma((NG - 1,)),
            dma((NY,)), dma((NY,)), dma((NY,)), dma((NY,)),
            dma((NY,)), dma((NY,)), dma((NY,)), dma((NY,)),
            dma((2, 2)), dma((2, 2)),
            dma((KT,)),
        ],
        compiler_params=pltpu.CompilerParams(
            collective_id=0, has_side_effects=True, vmem_limit_bytes=58 * 2**20
        ),
    )(
        starting_warmth_level,
        diffusive_coefficient_map,
        specific_warmth_store,
        energy_source_flux,
        deformation_vector,
        substance_label_columns,
        substance_moduli_table,
        subdomain_point_tally,
    )


def solution(mesh):
    placed = (
        P("gx", "yz", None),
        P("gx", "yz", None),
        P("gx", "yz", None),
        P("gx", "yz", None),
        P(None, "gx", "yz", None),
        P("gx", None),
        P(),
        P(),
    )
    return jax.shard_map(
        local,
        mesh=mesh,
        in_specs=placed,
        out_specs=(P("gx", "yz", None), P(None, "gx", None, "yz")),
        check_vma=False,
    )
```

time: 608 us -> 121 us (0.20); the launches traced: 596 us -> 120 us
  starting transfers between devices: 201 us -> 0 us
  local copies, waits for them, and re-layouts: 139 us -> 4.37 us
  blocking collectives: 134 us -> 0 us
  Pallas kernels: 0 us -> 115 us
  other arithmetic: 70.3 us -> 0 us
  waiting for transfers between devices: 44.9 us -> 0 us
    ppermute x56 -> x0, starting transfers between devices: 185 us -> none  [the longest x27 137 us: extended(): before = lax.ppermute(last, axis, up)]
    pallas_call x0 -> x1, Pallas kernels: none -> 115 us  [local(): pl.pallas_call(kernel, out_shape=(jax.ShapeDtypeStruct((B, B, KT * 128),...]
    pmax x1 -> x0, blocking collectives: 71 us -> none  [local(): high = lax.pmax(upper_local, ('gx', 'yz'))]
    pmin x1 -> x0, blocking collectives: 63.2 us -> none  [local(): low = lax.pmin(lower_local, ('gx', 'yz'))]
    unnamed x68 -> x2, local copies, waits for them, and re-layouts: 59.3 us -> 4.37 us
    gather x1 -> x0, local copies, waits for them, and re-layouts: 32.7 us -> none  [local(): sent = jnp.take(padded_field, where_from, axis=3) * valid]
    unnamed x1 -> x0, other arithmetic: 26.9 us -> none
    all_to_all x1 -> x0, waiting for transfers between devices: 23.7 us -> none  [local(): lax.all_to_all(sent, 'yz', split_axis=3, concat_axis=2, tiled=True)]
  transfers between devices with their start and end apart: 57 -> 0, of which waited for: 23 -> 0; matrix products, arithmetic and copies ran while one was open for 2% -> 0% of each run, Pallas kernels for 0% -> 0%
where the time goes in v1:
time: 121 us; the launch traced here: 120 us
  Pallas kernels  115 us (95%)
  local copies, waits for them, and re-layouts  4.37 us (4%)
    pallas_call x1, Pallas kernels, local(): pl.pallas_call(kernel, out_shape=(jax.ShapeDtypeStruct((B, B, KT * 128),...  115 us
    unnamed x2, local copies, waits for them, and re-layouts  4.37 us

profile of v1, /device:TPU:1, one launch (start us, length us, event | category | flops | bytes accessed | tf_op | source)
XLA Modules:
  0.0 120.2 jit_solution(8239251523206975083)
XLA Ops:
  0.6 115.1 %shard_map.95 = (f32[8,8,1024]{2,1,0:T(8,128)}, f32[3,8,128,128]{3,2,1,0:T(8,128)}) custom-call(f32[8,8,1024]{2,1,0:T(8,128)} %x0_hbm.1, f32[8,8,1024]{2,1,0:T(8,128)} %k_hbm.1, f32[8,8,1024]{2,1,0:T(8,128)} %c_hbm.1, f32[8,8,1024]{2,1,0:T(8,128)} %f_hbm.1, f32[3,8,8,1024]{3,2,1,0:T(8,128)} %u_hbm.1, s32[8,128]{1,0:T(8,128)} %lab.1, f32[2,2]{1,0:T(2,128)} %table.1, ...), custom_call_target="tpu_custom_call" | custom-call | tf_op jit(solution)/shard_map/pallas_call | solution.py:578
  115.8 1.7 %copy.12 = f32[8,8,1024]{2,1,0:T(8,128)} copy(f32[8,8,1024]{2,1,0:T(8,128)} %get-tuple-element.4) | data formatting | bytes 524288
  117.5 2.7 %copy.13 = f32[3,8,128,128]{3,2,1,0:T(8,128)} copy(f32[3,8,128,128]{3,2,1,0:T(8,128)} %get-tuple-element.5) | data formatting | bytes 3145728

commit v2 on v1

v2 whole, which is shorter than its diff:
```python
import functools

import jax
import jax.numpy as jnp
from jax import lax
from jax.experimental import pallas as pl
from jax.experimental.pallas import tpu as pltpu
from jax.sharding import PartitionSpec as P

NCHEB = 6
ZMAX = 128
NG, NY = 8, 16
B = 8
H = 6
N = B + 2 * H
LO, HI = H, H + B
KT = 8
LEVELS = NCHEB - 1
MESH = pl.DeviceIdType.MESH
F32 = jnp.float32


def corner_rects(width):
    if width == 6:
        return [(1, 2, 5), (3, 5, 3)]
    if width == 5:
        return [(1, 2, 4), (3, 4, 2)]
    return []


def kernel(
    x0_hbm, k_hbm, c_hbm, f_hbm, u_hbm, lab, table, tally,
    t_out, r_out,
    nat, natu, kb, cb, xb, fb, v0, v1, e, rb, fx, fy, fz, db,
    ust, uest, u, ue, tst, t, natt, ytr,
    mu, beta, ar1, ar2, arst, coefs, starts,
    lsem, lusem, hs, hr, a1s, a1r, a2s, a2r, us, ur, ues, uer, ts, tr, ps, pr, bs, br, osem,
):
    g, y = lax.axis_index("gx"), lax.axis_index("yz")
    gp, gm = lax.rem(g + 1, NG), lax.rem(g + NG - 1, NG)
    yp, ym = lax.rem(y + 1, NY), lax.rem(y + NY - 1, NY)
    along_y = [(g, lax.rem(y + k, NY)) for k in range(1, NY)]
    along_g = [(lax.rem(g + k, NG), y) for k in range(1, NG)]
    core = lax.rem(g, 2)
    sibling = (g + 1 - 2 * core, y)
    across = lax.rem(g + 2 * core - 1 + NG, NG)
    diagonal = [(across, yp), (across, ym)]

    fields = [k_hbm, x0_hbm, c_hbm, f_hbm]
    own_in = [
        [
            pltpu.make_async_copy(
                field.at[:, :, pl.ds(kt * 128, 128)], nat.at[n, :, pl.ds(kt * 8, 8)], lsem.at[n, kt]
            )
            for kt in range(KT)
        ]
        for n, field in enumerate(fields)
    ]
    u_in = [
        pltpu.make_async_copy(
            u_hbm.at[:, :, :, pl.ds(kt * 128, 128)], natu.at[:, :, kt + 1], lusem.at[kt]
        )
        for kt in range(KT)
    ]
    for copies in own_in:
        for copy in copies:
            copy.start()
    for copy in u_in:
        copy.start()

    barrier = pltpu.get_barrier_semaphore()
    for peer in along_y + along_g + diagonal:
        pl.semaphore_signal(barrier, inc=1, device_id=peer, device_id_type=MESH)

    zero_tile = jnp.zeros((8, 128), F32)
    for a in range(3):
        def zero_u(i, _, a=a):
            u[a, i, pl.ds(0, 8)] = zero_tile
            u[a, i, pl.ds(8 + 128, 8)] = zero_tile
            return 0
        lax.fori_loop(0, B + 2, zero_u, 0)

        def zero_natu(i, _, a=a):
            natu[a, i, 0] = zero_tile
            natu[a, i, KT + 1] = zero_tile
            return 0
        lax.fori_loop(0, B, zero_natu, 0)

    def zero_t(i, _):
        t[i, pl.ds(0, 8)] = zero_tile
        t[i, pl.ds(8 + 128, 8)] = zero_tile
        return 0
    lax.fori_loop(0, B + 2, zero_t, 0)

    def zero_natt(i, _):
        natt[i, 0] = zero_tile
        natt[i, KT + 1] = zero_tile
        return 0
    lax.fori_loop(0, B + 2, zero_natt, 0)

    def to_lines(n, dst):
        def row(i, _):
            for j in range(B):
                dst[LO + i, LO + j] = nat[n, i, pl.ds(j, 8, stride=8), :]
            return 0
        lax.fori_loop(0, B, row, 0)

    for n, dst in ((0, kb), (1, xb), (2, cb), (3, fb)):
        for copy in own_in[n]:
            copy.wait()
        to_lines(n, dst)

    pl.semaphore_wait(barrier, len(along_y) + len(along_g) + len(diagonal))

    def halo(buf, width, slot, width_j=None):
        def sides(w):
            return pl.ds(LO - w, w), pl.ds(HI, w), pl.ds(LO, w), pl.ds(HI - w, w)

        own = pl.ds(LO, B)
        low_i, high_i, first_i, last_i = sides(width)
        low_j, high_j, first_j, last_j = sides(width_j or width)
        moves = [
            (buf.at[own, last_j], buf.at[own, low_j], (g, yp)),
            (buf.at[own, first_j], buf.at[own, high_j], (g, ym)),
            (buf.at[last_i, own], buf.at[low_i, own], (gp, y)),
            (buf.at[first_i, own], buf.at[high_i, own], (gm, y)),
        ]
        relayed = []
        for a0, a1, b1 in corner_rects(width):
            rows = a1 - a0 + 1
            in_low, out_low, in_high, out_high = LO + a0 - 1, LO - a1, HI - a1, HI - 1 + a0
            to_across, at_across = in_low + core * (in_high - in_low), out_high + core * (out_low - out_high)
            to_sibling, at_sibling = in_high + core * (in_low - in_high), out_low + core * (out_high - out_low)
            low, high, first, last = (pl.ds(LO - b1, b1), pl.ds(HI, b1), pl.ds(LO, b1), pl.ds(HI - b1, b1))
            src, dst = pl.ds(to_across, rows), pl.ds(at_across, rows)
            moves += [
                (buf.at[src, last], buf.at[dst, low], diagonal[0]),
                (buf.at[src, first], buf.at[dst, high], diagonal[1]),
            ]
            src, dst = pl.ds(to_sibling, rows), pl.ds(at_sibling, rows)
            relayed += [(buf.at[src, low], buf.at[dst, low], sibling), (buf.at[src, high], buf.at[dst, high], sibling)]
        copies = [
            pltpu.make_async_remote_copy(
                src_ref=src, dst_ref=dst, send_sem=hs.at[slot, m], recv_sem=hr.at[slot, m],
                device_id=peer, device_id_type=MESH,
            )
            for m, (src, dst, peer) in enumerate(moves + relayed)
        ]
        return copies[:len(moves)], copies[len(moves):]

    def relay(moves, relayed):
        for copy in moves[:2]:
            copy.wait_recv()
        for copy in relayed:
            copy.start()
        for copy in moves[2:] + relayed:
            copy.wait_recv()

    def plane_copies(buf, at, send, recv):
        return [
            pltpu.make_async_remote_copy(
                src_ref=buf.at[at(B)], dst_ref=buf.at[at(0)],
                send_sem=send.at[0], recv_sem=recv.at[0], device_id=(gp, y), device_id_type=MESH,
            ),
            pltpu.make_async_remote_copy(
                src_ref=buf.at[at(1)], dst_ref=buf.at[at(B + 1)],
                send_sem=send.at[1], recv_sem=recv.at[1], device_id=(gm, y), device_id_type=MESH,
            ),
        ]

    x0_moves, _ = halo(xb, 1, 0)
    k_moves, k_relayed = halo(kb, 6, 1)
    c_moves, c_relayed = halo(cb, 5, 2)
    for copy in x0_moves + k_moves + c_moves:
        copy.start()

    total = jnp.int32(0)
    for p in range(NY):
        starts[p] = total
        total = total + tally[p]

    eye = lax.broadcasted_iota(jnp.int32, (128, 128), 0) == lax.broadcasted_iota(jnp.int32, (128, 128), 1)

    def column_row(i, _):
        row = jnp.broadcast_to(lab[pl.ds(i, 1), :].astype(F32), (128, 128))
        column = jnp.sum(jnp.where(eye, row, 0.0), axis=1, keepdims=True)
        label = jnp.broadcast_to(column, (128, 128))
        for dst, r, at in ((mu, 0, i), (beta, 1, i + 1)):
            dst[at] = jnp.where(label == 0.0, table[r, 0], 0.0) + jnp.where(label == 1.0, table[r, 1], 0.0)
        return 0
    lax.fori_loop(0, B, column_row, 0)
    beta_planes = plane_copies(beta, lambda i: (i,), bs, br)
    for copy in beta_planes:
        copy.start()

    lane = lax.broadcasted_iota(jnp.int32, (8, 128), 1)

    def cuts(p):
        start = starts[p]
        before, after = start + 127, start + tally[p] + 128
        return (start >> 7) + 1, start & 127, before >> 7, before & 127, after >> 7, after & 127

    def pack(line, cut, lane_of, edge):
        tile, off, tile_before, lane_before, tile_after, lane_after = cut
        window = jnp.where(lane >= off, line[tile], line[tile + 1])
        prev = pltpu.roll(line[tile_before], (lane_of - lane_before + 256) & 127, 1)
        nxt = pltpu.roll(line[tile_after], (32 + lane_of - lane_after + 256) & 127, 1)
        edge = jnp.where(lane == lane_of, prev, jnp.where(lane == lane_of + 32, nxt, edge))
        return pltpu.roll(window, (128 - off) & 127, 1), edge

    for copy in u_in:
        copy.wait()

    def pack_u(p, _):
        cut = cuts(p)
        edge = zero_tile
        for a in range(3):
            for i in range(B):
                ust[p, a, i], edge = pack(natu.at[a, i], cut, a * 8 + i, edge)
        uest[p] = edge
        return 0
    lax.fori_loop(0, NY, pack_u, 0)

    rows_of_me = pl.ds(pl.multiple_of(8 + 8 * y, 8), 8)

    def u_copies(k):
        p = lax.rem(y + k, NY)
        peer = (g, p)
        return [
            pltpu.make_async_remote_copy(
                src_ref=ust.at[p], dst_ref=u.at[:, pl.ds(1, B), rows_of_me],
                send_sem=us.at[k], recv_sem=ur.at[k], device_id=peer, device_id_type=MESH,
            ),
            pltpu.make_async_remote_copy(
                src_ref=uest.at[p], dst_ref=ue.at[rows_of_me],
                send_sem=ues.at[k], recv_sem=uer.at[k], device_id=peer, device_id_type=MESH,
            ),
        ]

    u_moves = [u_copies(k) for k in range(1, NY)]
    u_own = [
        pltpu.make_async_copy(ust.at[y], u.at[:, pl.ds(1, B), rows_of_me], us.at[0]),
        pltpu.make_async_copy(uest.at[y], ue.at[rows_of_me], ues.at[0]),
    ]
    def send_u(ks):
        for k in ks:
            for copy in u_moves[k - 1]:
                copy.start()

    send_u((4, 8, 12))
    for copy in u_own:
        copy.start()

    def iota(n, axis):
        return lax.broadcasted_iota(jnp.int32, (n, 8, 128), axis)

    def up(v):
        by_lane = pltpu.roll(v, 127, 2)
        return jnp.where(iota(v.shape[0], 2) == 127, pltpu.roll(by_lane, 7, 1), by_lane)

    def down(v):
        by_lane = pltpu.roll(v, 1, 2)
        return jnp.where(iota(v.shape[0], 2) == 0, pltpu.roll(by_lane, 1, 1), by_lane)

    def harmonic(first, second):
        return 2.0 * first * second / (first + second)

    inside_low_g = jnp.where(g > 0, 1.0, 0.0)
    inside_high_g = jnp.where(g < NG - 1, 1.0, 0.0)
    inside_low_y = jnp.where(y > 0, 1.0, 0.0)
    inside_high_y = jnp.where(y < NY - 1, 1.0, 0.0)

    def faces(q):
        lo, n = LO - q, B + 2 * q

        whole = pl.ds(lo, n)
        fx[lo - 1, whole] = harmonic(kb[lo - 1, whole], kb[lo, whole])

        def fx_rows(step, _):
            i = lo + 2 * step
            low, high = harmonic(kb[i, whole], kb[i + 1, whole]), harmonic(kb[i + 1, whole], kb[i + 2, whole])
            fx[i, whole] = low
            fx[i + 1, whole] = high
            return 0
        lax.fori_loop(0, n // 2, fx_rows, 0)

        fx[LO - 1, pl.ds(lo, n)] = fx[LO - 1, pl.ds(lo, n)] * inside_low_g
        fx[HI - 1, pl.ds(lo, n)] = fx[HI - 1, pl.ds(lo, n)] * inside_high_g

        last = (iota(n, 1) == 7) & (iota(n, 2) == 127)

        def rows(step, _):
            first = lo + 2 * step
            done = []
            for i in (first, first + 1):
                own = kb[i, whole]
                low = harmonic(kb[i, lo - 1], kb[i, lo])
                along_j = harmonic(own, kb[i, pl.ds(lo + 1, n)])
                along_k = jnp.where(last, 0.0, harmonic(own, up(own)))
                done.append((low, along_j, along_k, cb[i, whole] + fx[i, whole] + fx[i - 1, whole] + along_k + down(along_k)))
            for i, (low, along_j, along_k, others) in enumerate(done):
                i = first + i
                fy[i, lo - 1] = low
                fy[i, whole] = along_j
                fz[i, whole] = along_k
                db[i, whole] = others
            return 0
        lax.fori_loop(0, n // 2, rows, 0)

        span = pl.ds(lo, n)
        fy[span, LO - 1] = fy[span, LO - 1] * inside_low_y
        fy[span, HI - 1] = fy[span, HI - 1] * inside_high_y

        def diagonal_row(i, _):
            db[i, whole] = db[i, whole] + fy[i, whole] + fy[i, pl.ds(lo - 1, n)]
            return 0
        lax.fori_loop(lo, lo + n, diagonal_row, 0)

    def applied(v, i, j0, c):
        at = pl.ds(j0, c)
        own, z = v[i, at], fz[i, at]
        return (
            db[i, at] * own
            - fx[i, at] * v[i + 1, at]
            - fx[i - 1, at] * v[i - 1, at]
            - fy[i, at] * v[i, pl.ds(j0 + 1, c)]
            - fy[i, pl.ds(j0 - 1, c)] * v[i, pl.ds(j0 - 1, c)]
            - z * up(own)
            - down(z * own)
        )

    def first_residual(x, dst):
        at = pl.ds(LO, B)
        done = [fb[i, at] + (cb[i, at] * x[i, at] - applied(x, i, LO, B)) for i in range(LO, HI)]
        for i, value in enumerate(done):
            dst[LO + i, at] = value

    for copy in x0_moves + k_moves[:4]:
        copy.wait_recv()
    for copy in k_relayed:
        copy.start()
    faces(0)

    def bound_row(i, carry):
        most, least = carry
        at = pl.ds(LO, B)
        c = cb[i, at]
        return (
            jnp.maximum(most, jnp.max(2.0 * db[i, at] - c, axis=0)),
            jnp.maximum(least, jnp.max(-c, axis=0)),
        )
    neg = jnp.full((8, 128), -3.0e38, F32)
    most, least = lax.fori_loop(LO, HI, bound_row, (neg, neg))
    sub = lax.broadcasted_iota(jnp.int32, (8, 128), 0)

    def over_rows(v):
        return jnp.broadcast_to(jnp.max(v, axis=0, keepdims=True), (8, 128))

    arst[0] = jnp.where(sub < 4, over_rows(most), over_rows(least))
    ar1[y] = arst[0]
    ar1_moves = [
        pltpu.make_async_remote_copy(
            src_ref=arst.at[0], dst_ref=ar1.at[y], send_sem=a1s.at[k], recv_sem=a1r.at[k],
            device_id=peer, device_id_type=MESH,
        )
        for k, peer in enumerate(along_y)
    ]
    for copy in ar1_moves:
        copy.start()

    first_residual(xb, v0)
    v0_moves, v0_relayed = halo(v0, 6, 3)
    for copy in v0_moves:
        copy.start()

    relay(c_moves, c_relayed)
    for copy in k_moves[4:] + k_relayed:
        copy.wait_recv()
    faces(5)

    for copy in ar1_moves:
        copy.wait_recv()
    arst[1] = jnp.max(ar1[...], axis=0)
    ar2[g] = arst[1]
    ar2_moves = [
        pltpu.make_async_remote_copy(
            src_ref=arst.at[1], dst_ref=ar2.at[g], send_sem=a2s.at[k], recv_sem=a2r.at[k],
            device_id=peer, device_id_type=MESH,
        )
        for k, peer in enumerate(along_g)
    ]
    for copy in ar2_moves:
        copy.start()
    for copy in ar2_moves:
        copy.wait_recv()
    bounds = jnp.max(jnp.max(ar2[...], axis=0), axis=1, keepdims=True)
    high = jnp.broadcast_to(bounds[0:1], (8, 128))
    low = -jnp.broadcast_to(bounds[4:5], (8, 128))
    theta = (high + low) / 2.0
    delta = (high - low) / 2.0
    sigma = theta / delta
    rho = 1.0 / sigma
    coefs[0] = 1.0 / theta
    for turn in range(LEVELS):
        rho_new = 1.0 / (2.0 * sigma - rho)
        coefs[1 + 2 * turn] = rho_new * rho
        coefs[2 + 2 * turn] = 2.0 * rho_new / delta * theta
        rho = rho_new

    def level(src, turn, qi, qj):
        lo, n = LO - qi, B + 2 * qi
        rows = max(d for d in range(1, 10) if n % d == 0)
        j0, c = LO - qj, B + 2 * qj
        at = pl.ds(j0, c)
        inv, alpha, bet = coefs[0], coefs[1 + 2 * turn], coefs[2 + 2 * turn]
        before = src if turn == 0 else rb

        def some_rows(step, _):
            first = lo + step * rows
            done = []
            for i in range(rows):
                resid = before[first + i, at] - inv[None] * applied(src, first + i, j0, c)
                done.append((resid, alpha[None] * src[first + i, at] + bet[None] * resid))
            for i, (resid, value) in enumerate(done):
                rb[first + i, at] = resid
                e[turn, first + i, at] = value
            return 0
        lax.fori_loop(0, n // rows, some_rows, 0)

    def heat_step(start, qi, qj):
        src = start
        for turn in range(LEVELS):
            level(src, turn, qi - 1 - turn, qj - 1 - turn)
            src = e.at[turn]

    def summed(start, i, at):
        total = start[i, at]
        for turn in range(LEVELS):
            total = total + e[turn, i, at]
        return xb[i, at] + coefs[0][None] * total

    relay(v0_moves, v0_relayed)
    send_u((1, 3, 5, 7, 9, 11))
    heat_step(v0, 6, 6)

    for copy in x0_moves:
        copy.wait_send()

    def next_x(i, _):
        at = pl.ds(LO - 1, B + 2)
        xb[i, at] = summed(v0, i, at)
        return 0
    lax.fori_loop(LO - 1, HI + 1, next_x, 0)

    first_residual(xb, v1)
    v1_moves, v1_relayed = halo(v1, 6, 4, 5)
    for copy in v1_moves:
        copy.start()
    send_u((13, 15, 2, 6, 10, 14))
    relay(v1_moves, v1_relayed)
    heat_step(v1, 6, 5)

    def last_x(i, _):
        final = summed(v1, LO - 1 + i, pl.ds(LO, B))
        for j in range(B):
            ytr[i, pl.ds(j * 8, 8)] = final[j]
        return 0
    lax.fori_loop(0, B + 2, last_x, 0)

    def to_natural(i, _):
        for kt in range(KT):
            natt[i, kt + 1] = ytr[i, pl.ds(kt, 8, stride=8), :]
        return 0
    lax.fori_loop(0, B + 2, to_natural, 0)

    t_copies_out = [
        pltpu.make_async_copy(natt.at[pl.ds(1, B), kt + 1], t_out.at[:, :, pl.ds(kt * 128, 128)], osem.at[kt])
        for kt in range(KT)
    ]
    for copy in t_copies_out:
        copy.start()

    def t_copies(k):
        p = lax.rem(y + k, NY)
        peer = (g, p)
        return [
            pltpu.make_async_remote_copy(
                src_ref=tst.at[p], dst_ref=t.at[:, rows_of_me],
                send_sem=ts.at[k], recv_sem=tr.at[k], device_id=peer, device_id_type=MESH,
            )
        ]

    t_moves = [t_copies(k) for k in range(1, NY)]
    t_own = [
        pltpu.make_async_copy(tst.at[y], t.at[:, rows_of_me], ts.at[0]),
    ]
    for group in ((10, 6, 9, 11), (14, 2, 5, 7), (13, 15, 8, 3), (1, 4, 12, 0)):
        done = []
        for k in group:
            p = lax.rem(y + k, NY)
            cut = cuts(p)
            edge = zero_tile
            windows = []
            for i in range(B + 2):
                window, edge = pack(natt.at[i], cut, i, edge)
                windows.append(window)
            done.append((k, p, windows + [edge]))
        for k, p, windows in done:
            for i, window in enumerate(windows):
                tst[p, i] = window
            for copy in t_own if k == 0 else t_moves[k - 1]:
                copy.start()

    for copy in u_own:
        copy.wait()
    for copies in u_moves:
        for copy in copies:
            copy.wait_recv()
    inner = pl.ds(8, 128)

    u_planes = plane_copies(u, lambda i: (slice(None), i, inner), ps, pr)
    for copy in u_planes:
        copy.start()

    length = tally[y]
    wide_lane = lax.broadcasted_iota(jnp.int32, (128, 128), 1)
    valid = wide_lane < length

    def beside(own, edges, at):
        nxt = pltpu.roll(edges, (length - 1 - 32 - at + 256) & 127, 1)
        prev = pltpu.roll(edges, (128 - at) & 127, 1)
        plus = jnp.where(wide_lane == length - 1, nxt, pltpu.roll(own, 127, 1))
        minus = jnp.where(wide_lane == 0, prev, pltpu.roll(own, 1, 1))
        return plus, minus

    for copy in u_planes:
        copy.wait_recv()
    for a in range(3):
        u[a, 0, inner] = u[a, 0, inner] * inside_low_g
        u[a, B + 1, inner] = u[a, B + 1, inner] * inside_high_g

        def disp_row(i, _, a=a):
            own = u[a, i + 1, inner]
            plus, minus = beside(own, ue[inner], a * 8 + i)
            total = (
                u[a, i + 2, inner] + u[a, i, inner] + u[a, i + 1, pl.ds(9, 128)] + u[a, i + 1, pl.ds(7, 128)]
                + plus + minus
            )
            r_out[a, i] = mu[i] * (6.0 * own - total)
            return 0
        lax.fori_loop(0, B, disp_row, 0)

    for copy in t_own:
        copy.wait()
    for copies in t_moves:
        for copy in copies:
            copy.wait_recv()

    for copy in beta_planes:
        copy.wait_recv()
    beta[0] = beta[0] * inside_low_g
    beta[B + 1] = beta[B + 1] * inside_high_g

    def stress_row(i, _):
        t[i, inner] = beta[i] * t[i, inner]
        return 0
    lax.fori_loop(0, B + 2, stress_row, 0)

    def stress_part(i, _):
        plus, minus = beside(t[i + 1, inner], beta[i + 1] * t[B + 2, inner], i + 1)
        along_i = t[i + 2, inner] - t[i, inner]
        along_j = t[i + 1, pl.ds(9, 128)] - t[i + 1, pl.ds(7, 128)]
        r_out[0, i] = jnp.where(valid, r_out[0, i] + 0.5 * along_i, 0.0)
        r_out[1, i] = jnp.where(valid, r_out[1, i] + 0.5 * along_j, 0.0)
        r_out[2, i] = jnp.where(valid, r_out[2, i] + 0.5 * (plus - minus), 0.0)
        return 0
    lax.fori_loop(0, B, stress_part, 0)

    for copy in k_moves + k_relayed + c_moves + c_relayed + v0_moves + v0_relayed + v1_moves + v1_relayed:
        copy.wait_send()
    for copy in ar1_moves + ar2_moves + u_planes + beta_planes:
        copy.wait_send()
    for copies in u_moves + t_moves:
        for copy in copies:
            copy.wait_send()
    for copy in t_copies_out:
        copy.wait()


def local(
    starting_warmth_level,
    diffusive_coefficient_map,
    specific_warmth_store,
    energy_source_flux,
    deformation_vector,
    substance_label_columns,
    substance_moduli_table,
    subdomain_point_tally,
):
    hbm = pl.BlockSpec(memory_space=pl.ANY)
    vmem = pl.BlockSpec(memory_space=pltpu.VMEM)
    smem = pl.BlockSpec(memory_space=pltpu.SMEM)
    grid = pltpu.VMEM((N, N, 8, 128), F32)
    dma = pltpu.SemaphoreType.DMA
    return pl.pallas_call(
        kernel,
        out_shape=(
            jax.ShapeDtypeStruct((B, B, KT * 128), F32),
            jax.ShapeDtypeStruct((3, B, NY * 8, ZMAX), F32),
        ),
        in_specs=[hbm] * 5 + [vmem, smem, smem],
        out_specs=(hbm, vmem),
        scratch_shapes=[
            pltpu.VMEM((4, B, KT * 8, 128), F32),
            pltpu.VMEM((3, B, KT + 2, 8, 128), F32),
            grid, grid, grid, grid, grid, grid,
            pltpu.VMEM((LEVELS, N, N, 8, 128), F32),
            grid, grid, grid, grid, grid,
            pltpu.VMEM((NY, 3, B, 8, 128), F32),
            pltpu.VMEM((NY, 8, 128), F32),
            pltpu.VMEM((3, B + 2, 8 + 128 + 8, 128), F32),
            pltpu.VMEM((8 + 128 + 8, 128), F32),
            pltpu.VMEM((NY, B + 3, 8, 128), F32),
            pltpu.VMEM((B + 3, 8 + 128 + 8, 128), F32),
            pltpu.VMEM((B + 2, KT + 2, 8, 128), F32),
            pltpu.VMEM((B + 2, B * 8, 128), F32),
            pltpu.VMEM((B, 128, 128), F32),
            pltpu.VMEM((B + 2, 128, 128), F32),
            pltpu.VMEM((NY, 8, 128), F32),
            pltpu.VMEM((NG, 8, 128), F32),
            pltpu.VMEM((2, 8, 128), F32),
            pltpu.VMEM((1 + 2 * LEVELS, 8, 128), F32),
            pltpu.SMEM((NY,), jnp.int32),
            dma((4, KT)), dma((KT,)),
            dma((5, 12)), dma((5, 12)),
            dma((NY - 1,)), dma((NY - 1,)), dma((NG - 1,)), dma((NG - 1,)),
            dma((NY,)), dma((NY,)), dma((NY,)), dma((NY,)),
            dma((NY,)), dma((NY,)),
            dma((2,)), dma((2,)), dma((2,)), dma((2,)),
            dma((KT,)),
        ],
        compiler_params=pltpu.CompilerParams(
            collective_id=0, has_side_effects=True, vmem_limit_bytes=58 * 2**20
        ),
    )(
        starting_warmth_level,
        diffusive_coefficient_map,
        specific_warmth_store,
        energy_source_flux,
        deformation_vector,
        substance_label_columns,
        substance_moduli_table,
        subdomain_point_tally,
    )


def solution(mesh):
    placed = (
        P("gx", "yz", None),
        P("gx", "yz", None),
        P("gx", "yz", None),
        P("gx", "yz", None),
        P(None, "gx", "yz", None),
        P("gx", None),
        P(),
        P(),
    )
    return jax.shard_map(
        local,
        mesh=mesh,
        in_specs=placed,
        out_specs=(P("gx", "yz", None), P(None, "gx", None, "yz")),
        check_vma=False,
    )
```

time: 121 us -> 84.5 us (0.70)
  Pallas kernels: 115 us -> 79.2 us
    pallas_call x1, Pallas kernels: 115 us -> 79.2 us  [local(): pl.pallas_call(kernel, out_shape=(jax.ShapeDtypeStruct((B, B, KT * 128),...]
where the time goes in v2:
time: 84.5 us; the launch traced here: 84.3 us
  Pallas kernels  79.2 us (94%)
  local copies, waits for them, and re-layouts  4.37 us (5%)
    pallas_call x1, Pallas kernels, local(): pl.pallas_call(kernel, out_shape=(jax.ShapeDtypeStruct((B, B, KT * 128),...  79.2 us
    unnamed x2, local copies, waits for them, and re-layouts  4.37 us

profile of v2, /device:TPU:1, one launch (start us, length us, event | category | flops | bytes accessed | tf_op | source)
XLA Modules:
  0.0 84.3 jit_solution(10069988307173718426)
XLA Ops:
  0.6 79.2 %shard_map.95 = (f32[8,8,1024]{2,1,0:T(8,128)}, f32[3,8,128,128]{3,2,1,0:T(8,128)}) custom-call(f32[8,8,1024]{2,1,0:T(8,128)} %x0_hbm.1, f32[8,8,1024]{2,1,0:T(8,128)} %k_hbm.1, f32[8,8,1024]{2,1,0:T(8,128)} %c_hbm.1, f32[8,8,1024]{2,1,0:T(8,128)} %f_hbm.1, f32[3,8,8,1024]{3,2,1,0:T(8,128)} %u_hbm.1, s32[8,128]{1,0:T(8,128)} %lab.1, f32[2,2]{1,0:T(2,128)} %table.1, ...), custom_call_target="tpu_custom_call" | custom-call | tf_op jit(solution)/shard_map/pallas_call | solution.py:605
  79.9 1.7 %copy.12 = f32[8,8,1024]{2,1,0:T(8,128)} copy(f32[8,8,1024]{2,1,0:T(8,128)} %get-tuple-element.4) | data formatting | bytes 524288
  81.6 2.7 %copy.13 = f32[3,8,128,128]{3,2,1,0:T(8,128)} copy(f32[3,8,128,128]{3,2,1,0:T(8,128)} %get-tuple-element.5) | data formatting | bytes 3145728

commit v3 on v2

--- a/solution.py
+++ b/solution.py
@@ -34,7 +34,7 @@
     nat, natu, kb, cb, xb, fb, v0, v1, e, rb, fx, fy, fz, db,
     ust, uest, u, ue, tst, t, natt, ytr,
     mu, beta, ar1, ar2, arst, coefs, starts,
-    lsem, lusem, hs, hr, a1s, a1r, a2s, a2r, us, ur, ues, uer, ts, tr, ps, pr, bs, br, osem,
+    lsem, lusem, hs, hr, a1s, a1r, a2s, a2r, us, ur, ues, uer, ts, tr, ps, pr, bs, br,
 ):
     g, y = lax.axis_index("gx"), lax.axis_index("yz")
     gp, gm = lax.rem(g + 1, NG), lax.rem(g + NG - 1, NG)
@@ -148,11 +148,14 @@
         ]
         return copies[:len(moves)], copies[len(moves):]
 
-    def relay(moves, relayed):
+    def relay_start(moves, relayed):
         for copy in moves[:2]:
             copy.wait_recv()
         for copy in relayed:
             copy.start()
+
+    def relay(moves, relayed):
+        relay_start(moves, relayed)
         for copy in moves[2:] + relayed:
             copy.wait_recv()
 
@@ -373,11 +376,8 @@
     for copy in v0_moves:
         copy.start()
 
-    relay(c_moves, c_relayed)
-    for copy in k_moves[4:] + k_relayed:
-        copy.wait_recv()
-    faces(5)
-
+    send_u((1, 3, 5, 7, 9, 11))
+    relay_start(c_moves, c_relayed)
     for copy in ar1_moves:
         copy.wait_recv()
     arst[1] = jnp.max(ar1[...], axis=0)
@@ -391,8 +391,18 @@
     ]
     for copy in ar2_moves:
         copy.start()
+    for copy in c_moves[2:] + c_relayed + k_moves[4:] + k_relayed:
+        copy.wait_recv()
+    faces(5)
+
     for copy in ar2_moves:
         copy.wait_recv()
+    send_u((13, 15, 2, 6, 10, 14))
+    for copy in beta_planes:
+        copy.wait()
+    beta[0] = beta[0] * inside_low_g
+    beta[B + 1] = beta[B + 1] * inside_high_g
+
     bounds = jnp.max(jnp.max(ar2[...], axis=0), axis=1, keepdims=True)
     high = jnp.broadcast_to(bounds[0:1], (8, 128))
     low = -jnp.broadcast_to(bounds[4:5], (8, 128))
@@ -440,7 +450,6 @@
         return xb[i, at] + coefs[0][None] * total
 
     relay(v0_moves, v0_relayed)
-    send_u((1, 3, 5, 7, 9, 11))
     heat_step(v0, 6, 6)
 
     for copy in x0_moves:
@@ -456,7 +465,6 @@
     v1_moves, v1_relayed = halo(v1, 6, 4, 5)
     for copy in v1_moves:
         copy.start()
-    send_u((13, 15, 2, 6, 10, 14))
     relay(v1_moves, v1_relayed)
     heat_step(v1, 6, 5)
 
@@ -473,12 +481,8 @@
         return 0
     lax.fori_loop(0, B + 2, to_natural, 0)
 
-    t_copies_out = [
-        pltpu.make_async_copy(natt.at[pl.ds(1, B), kt + 1], t_out.at[:, :, pl.ds(kt * 128, 128)], osem.at[kt])
-        for kt in range(KT)
-    ]
-    for copy in t_copies_out:
-        copy.start()
+    for kt in range(KT):
+        t_out[:, :, pl.ds(kt * 128, 128)] = natt[pl.ds(1, B), kt + 1]
 
     def t_copies(k):
         p = lax.rem(y + k, NY)
@@ -524,31 +528,36 @@
 
     length = tally[y]
     wide_lane = lax.broadcasted_iota(jnp.int32, (128, 128), 1)
-    valid = wide_lane < length
-
-    def beside(own, edges, at):
-        nxt = pltpu.roll(edges, (length - 1 - 32 - at + 256) & 127, 1)
-        prev = pltpu.roll(edges, (128 - at) & 127, 1)
-        plus = jnp.where(wide_lane == length - 1, nxt, pltpu.roll(own, 127, 1))
-        minus = jnp.where(wide_lane == 0, prev, pltpu.roll(own, 1, 1))
-        return plus, minus
+    edges = ue[inner]
+
+    def disp(a, i):
+        own = u[a, i + 1, inner]
+        plus, minus = beside(own, edges, a * 8 + i, length, wide_lane)
+        total = (
+            u[a, i + 2, inner] + u[a, i, inner] + u[a, i + 1, pl.ds(9, 128)] + u[a, i + 1, pl.ds(7, 128)]
+            + plus + minus
+        )
+        return mu[i] * (6.0 * own - total)
+
+    for a in range(3):
+        def disp_rows(step, _, a=a):
+            first = 1 + 2 * step
+            done = [disp(a, first), disp(a, first + 1)]
+            for i, value in enumerate(done):
+                r_out[a, first + i] = value
+            return 0
+        lax.fori_loop(0, B // 2 - 1, disp_rows, 0)
 
     for copy in u_planes:
         copy.wait_recv()
     for a in range(3):
         u[a, 0, inner] = u[a, 0, inner] * inside_low_g
         u[a, B + 1, inner] = u[a, B + 1, inner] * inside_high_g
-
-        def disp_row(i, _, a=a):
-            own = u[a, i + 1, inner]
-            plus, minus = beside(own, ue[inner], a * 8 + i)
-            total = (
-                u[a, i + 2, inner] + u[a, i, inner] + u[a, i + 1, pl.ds(9, 128)] + u[a, i + 1, pl.ds(7, 128)]
-                + plus + minus
-            )
-            r_out[a, i] = mu[i] * (6.0 * own - total)
-            return 0
-        lax.fori_loop(0, B, disp_row, 0)
+        done = [disp(a, 0), disp(a, B - 1)]
+        r_out[a, 0] = done[0]
+        r_out[a, B - 1] = done[1]
+
+    valid = wide_lane < length
 
     for copy in t_own:
         copy.wait()
@@ -556,35 +565,37 @@
         for copy in copies:
             copy.wait_recv()
 
-    for copy in beta_planes:
-        copy.wait_recv()
-    beta[0] = beta[0] * inside_low_g
-    beta[B + 1] = beta[B + 1] * inside_high_g
-
-    def stress_row(i, _):
+    for i in range(B + 2):
         t[i, inner] = beta[i] * t[i, inner]
-        return 0
-    lax.fori_loop(0, B + 2, stress_row, 0)
-
-    def stress_part(i, _):
-        plus, minus = beside(t[i + 1, inner], beta[i + 1] * t[B + 2, inner], i + 1)
-        along_i = t[i + 2, inner] - t[i, inner]
-        along_j = t[i + 1, pl.ds(9, 128)] - t[i + 1, pl.ds(7, 128)]
-        r_out[0, i] = jnp.where(valid, r_out[0, i] + 0.5 * along_i, 0.0)
-        r_out[1, i] = jnp.where(valid, r_out[1, i] + 0.5 * along_j, 0.0)
-        r_out[2, i] = jnp.where(valid, r_out[2, i] + 0.5 * (plus - minus), 0.0)
-        return 0
-    lax.fori_loop(0, B, stress_part, 0)
+
+    def stress_rows(step, _):
+        done = []
+        for i in (2 * step, 2 * step + 1):
+            plus, minus = beside(t[i + 1, inner], beta[i + 1] * t[B + 2, inner], i + 1, length, wide_lane)
+            along_i = t[i + 2, inner] - t[i, inner]
+            along_j = t[i + 1, pl.ds(9, 128)] - t[i + 1, pl.ds(7, 128)]
+            for a, v in enumerate((along_i, along_j, plus - minus)):
+                done.append((a, i, jnp.where(valid, r_out[a, i] + 0.5 * v, 0.0)))
+        for a, i, value in done:
+            r_out[a, i] = value
+        return 0
+    lax.fori_loop(0, B // 2, stress_rows, 0)
 
     for copy in k_moves + k_relayed + c_moves + c_relayed + v0_moves + v0_relayed + v1_moves + v1_relayed:
         copy.wait_send()
-    for copy in ar1_moves + ar2_moves + u_planes + beta_planes:
+    for copy in ar1_moves + ar2_moves + u_planes:
         copy.wait_send()
     for copies in u_moves + t_moves:
         for copy in copies:
             copy.wait_send()
-    for copy in t_copies_out:
-        copy.wait()
+
+
+def beside(own, edges, at, length, lane):
+    nxt = pltpu.roll(edges, (length - 1 - 32 - at + 256) & 127, 1)
+    prev = pltpu.roll(edges, (128 - at) & 127, 1)
+    plus = jnp.where(lane == length - 1, nxt, pltpu.roll(own, 127, 1))
+    minus = jnp.where(lane == 0, prev, pltpu.roll(own, 1, 1))
+    return plus, minus
 
 
 def local(
@@ -605,11 +616,11 @@
     return pl.pallas_call(
         kernel,
         out_shape=(
-            jax.ShapeDtypeStruct((B, B, KT * 128), F32),
-            jax.ShapeDtypeStruct((3, B, NY * 8, ZMAX), F32),
+            pltpu.VMEM((B, B, KT * 128), F32),
+            pltpu.VMEM((3, B, NY * 8, ZMAX), F32),
         ),
         in_specs=[hbm] * 5 + [vmem, smem, smem],
-        out_specs=(hbm, vmem),
+        out_specs=(vmem, vmem),
         scratch_shapes=[
             pltpu.VMEM((4, B, KT * 8, 128), F32),
             pltpu.VMEM((3, B, KT + 2, 8, 128), F32),
@@ -637,10 +648,9 @@
             dma((NY,)), dma((NY,)), dma((NY,)), dma((NY,)),
             dma((NY,)), dma((NY,)),
             dma((2,)), dma((2,)), dma((2,)), dma((2,)),
-            dma((KT,)),
         ],
         compiler_params=pltpu.CompilerParams(
-            collective_id=0, has_side_effects=True, vmem_limit_bytes=58 * 2**20
+            collective_id=0, has_side_effects=True, vmem_limit_bytes=60 * 2**20
         ),
     )(
         starting_warmth_level,

time: 84.5 us -> 76.3 us (0.903)
  Pallas kernels: 79.2 us -> 73.6 us
  local copies, waits for them, and re-layouts: 4.37 us -> 1.85 us
    pallas_call x1, Pallas kernels: 79.2 us -> 73.6 us  [local(): pl.pallas_call(kernel, out_shape=(pltpu.VMEM((B, B, KT * 128), F32), pltp...]
    unnamed x2, local copies, waits for them, and re-layouts: 4.37 us -> 1.85 us
where the time goes in v3:
time: 76.3 us; the launch traced here: 76.1 us
  Pallas kernels  73.6 us (96%)
  local copies, waits for them, and re-layouts  1.85 us (2%)
    pallas_call x1, Pallas kernels, local(): pl.pallas_call(kernel, out_shape=(pltpu.VMEM((B, B, KT * 128), F32), pltp...  73.6 us
    unnamed x2, local copies, waits for them, and re-layouts  1.85 us

profile of v3, /device:TPU:1, one launch (start us, length us, event | category | flops | bytes accessed | tf_op | source)
XLA Modules:
  0.0 76.1 jit_solution(304397070769734719)
XLA Ops:
  0.6 73.6 %shard_map.95 = (f32[8,8,1024]{2,1,0:T(8,128)S(1)}, f32[3,8,128,128]{3,2,1,0:T(8,128)S(1)}) custom-call(f32[8,8,1024]{2,1,0:T(8,128)} %x0_hbm.1, f32[8,8,1024]{2,1,0:T(8,128)} %k_hbm.1, f32[8,8,1024]{2,1,0:T(8,128)} %c_hbm.1, f32[8,8,1024]{2,1,0:T(8,128)} %f_hbm.1, f32[3,8,8,1024]{3,2,1,0:T(8,128)} %u_hbm.1, s32[8,128]{1,0:T(8,128)} %lab.1, f32[2,2]{1,0:T(2,128)} %table.1, ...), custom_call_target="tpu_custom_call" | custom-call | tf_op jit(solution)/shard_map/pallas_call | solution.py:616
  74.3 0.7 copy.12
  75.0 1.1 %copy.13 = f32[3,8,128,128]{3,2,1,0:T(8,128)} copy(f32[3,8,128,128]{3,2,1,0:T(8,128)S(1)} %get-tuple-element.3) | data formatting | bytes 3145728

commit v4 on v3

--- a/solution.py
+++ b/solution.py
@@ -39,7 +39,10 @@
     g, y = lax.axis_index("gx"), lax.axis_index("yz")
     gp, gm = lax.rem(g + 1, NG), lax.rem(g + NG - 1, NG)
     yp, ym = lax.rem(y + 1, NY), lax.rem(y + NY - 1, NY)
-    along_y = [(g, lax.rem(y + k, NY)) for k in range(1, NY)]
+    def shifted(k):
+        return lax.rem(y // 4 + k // 4, 4) * 4 + lax.rem(y + k % 4, 4)
+
+    along_y = [(g, shifted(k)) for k in range(1, NY)]
     along_g = [(lax.rem(g + k, NG), y) for k in range(1, NG)]
     core = lax.rem(g, 2)
     sibling = (g + 1 - 2 * core, y)
@@ -154,8 +157,9 @@
         for copy in relayed:
             copy.start()
 
-    def relay(moves, relayed):
+    def relay(moves, relayed, ks):
         relay_start(moves, relayed)
+        send_u(ks)
         for copy in moves[2:] + relayed:
             copy.wait_recv()
 
@@ -227,7 +231,7 @@
     rows_of_me = pl.ds(pl.multiple_of(8 + 8 * y, 8), 8)
 
     def u_copies(k):
-        p = lax.rem(y + k, NY)
+        p = shifted(k)
         peer = (g, p)
         return [
             pltpu.make_async_remote_copy(
@@ -250,7 +254,7 @@
             for copy in u_moves[k - 1]:
                 copy.start()
 
-    send_u((4, 8, 12))
+    send_u((4, 12, 8))
     for copy in u_own:
         copy.start()
 
@@ -376,7 +380,7 @@
     for copy in v0_moves:
         copy.start()
 
-    send_u((1, 3, 5, 7, 9, 11))
+    send_u((1, 3, 5, 15))
     relay_start(c_moves, c_relayed)
     for copy in ar1_moves:
         copy.wait_recv()
@@ -397,7 +401,7 @@
 
     for copy in ar2_moves:
         copy.wait_recv()
-    send_u((13, 15, 2, 6, 10, 14))
+    send_u((7, 13, 2, 10))
     for copy in beta_planes:
         copy.wait()
     beta[0] = beta[0] * inside_low_g
@@ -449,7 +453,7 @@
             total = total + e[turn, i, at]
         return xb[i, at] + coefs[0][None] * total
 
-    relay(v0_moves, v0_relayed)
+    relay(v0_moves, v0_relayed, (9, 11))
     heat_step(v0, 6, 6)
 
     for copy in x0_moves:
@@ -465,7 +469,7 @@
     v1_moves, v1_relayed = halo(v1, 6, 4, 5)
     for copy in v1_moves:
         copy.start()
-    relay(v1_moves, v1_relayed)
+    relay(v1_moves, v1_relayed, (6, 14))
     heat_step(v1, 6, 5)
 
     def last_x(i, _):
@@ -485,7 +489,7 @@
         t_out[:, :, pl.ds(kt * 128, 128)] = natt[pl.ds(1, B), kt + 1]
 
     def t_copies(k):
-        p = lax.rem(y + k, NY)
+        p = shifted(k)
         peer = (g, p)
         return [
             pltpu.make_async_remote_copy(
@@ -501,7 +505,7 @@
     for group in ((10, 6, 9, 11), (14, 2, 5, 7), (13, 15, 8, 3), (1, 4, 12, 0)):
         done = []
         for k in group:
-            p = lax.rem(y + k, NY)
+            p = shifted(k)
             cut = cuts(p)
             edge = zero_tile
             windows = []

time: 76.3 us -> 71.7 us (0.940)
  Pallas kernels: 73.6 us -> 69 us
    pallas_call x1, Pallas kernels: 73.6 us -> 69 us  [local(): pl.pallas_call(kernel, out_shape=(pltpu.VMEM((B, B, KT * 128), F32), pltp...]
where the time goes in v4:
time: 71.7 us; the launch traced here: 71.5 us
  Pallas kernels  69 us (96%)
  local copies, waits for them, and re-layouts  1.85 us (3%)
    pallas_call x1, Pallas kernels, local(): pl.pallas_call(kernel, out_shape=(pltpu.VMEM((B, B, KT * 128), F32), pltp...  69 us
    unnamed x2, local copies, waits for them, and re-layouts  1.85 us

profile of v4, /device:TPU:1, one launch (start us, length us, event | category | flops | bytes accessed | tf_op | source)
XLA Modules:
  0.0 71.5 jit_solution(12047794135036028499)
XLA Ops:
  0.6 69.0 %shard_map.95 = (f32[8,8,1024]{2,1,0:T(8,128)S(1)}, f32[3,8,128,128]{3,2,1,0:T(8,128)S(1)}) custom-call(f32[8,8,1024]{2,1,0:T(8,128)} %x0_hbm.1, f32[8,8,1024]{2,1,0:T(8,128)} %k_hbm.1, f32[8,8,1024]{2,1,0:T(8,128)} %c_hbm.1, f32[8,8,1024]{2,1,0:T(8,128)} %f_hbm.1, f32[3,8,8,1024]{3,2,1,0:T(8,128)} %u_hbm.1, s32[8,128]{1,0:T(8,128)} %lab.1, f32[2,2]{1,0:T(2,128)} %table.1, ...), custom_call_target="tpu_custom_call" | custom-call | tf_op jit(solution)/shard_map/pallas_call | solution.py:620
  69.7 0.7 copy.12
  70.4 1.1 %copy.13 = f32[3,8,128,128]{3,2,1,0:T(8,128)} copy(f32[3,8,128,128]{3,2,1,0:T(8,128)S(1)} %get-tuple-element.3) | data formatting | bytes 3145728

commit v5 on v4

--- a/solution.py
+++ b/solution.py
@@ -423,7 +423,7 @@
 
     def level(src, turn, qi, qj):
         lo, n = LO - qi, B + 2 * qi
-        rows = max(d for d in range(1, 10) if n % d == 0)
+        rows = max(d for d in range(1, 19) if n % d == 0)
         j0, c = LO - qj, B + 2 * qj
         at = pl.ds(j0, c)
         inv, alpha, bet = coefs[0], coefs[1 + 2 * turn], coefs[2 + 2 * turn]
@@ -459,11 +459,9 @@
     for copy in x0_moves:
         copy.wait_send()
 
-    def next_x(i, _):
+    for i in range(LO - 1, HI + 1):
         at = pl.ds(LO - 1, B + 2)
         xb[i, at] = summed(v0, i, at)
-        return 0
-    lax.fori_loop(LO - 1, HI + 1, next_x, 0)
 
     first_residual(xb, v1)
     v1_moves, v1_relayed = halo(v1, 6, 4, 5)
@@ -472,21 +470,11 @@
     relay(v1_moves, v1_relayed, (6, 14))
     heat_step(v1, 6, 5)
 
-    def last_x(i, _):
-        final = summed(v1, LO - 1 + i, pl.ds(LO, B))
-        for j in range(B):
-            ytr[i, pl.ds(j * 8, 8)] = final[j]
-        return 0
-    lax.fori_loop(0, B + 2, last_x, 0)
-
-    def to_natural(i, _):
+    for i in range(B + 2):
+        ytr[i] = summed(v1, LO - 1 + i, pl.ds(LO, B)).reshape(B * 8, 128)
+    for i in range(B + 2):
         for kt in range(KT):
             natt[i, kt + 1] = ytr[i, pl.ds(kt, 8, stride=8), :]
-        return 0
-    lax.fori_loop(0, B + 2, to_natural, 0)
-
-    for kt in range(KT):
-        t_out[:, :, pl.ds(kt * 128, 128)] = natt[pl.ds(1, B), kt + 1]
 
     def t_copies(k):
         p = shifted(k)
@@ -518,6 +506,9 @@
                 tst[p, i] = window
             for copy in t_own if k == 0 else t_moves[k - 1]:
                 copy.start()
+
+    for kt in range(KT):
+        t_out[:, :, pl.ds(kt * 128, 128)] = natt[pl.ds(1, B), kt + 1]
 
     for copy in u_own:
         copy.wait()

time: 71.7 us -> 71 us (level)
    pallas_call x1, Pallas kernels: 69 us -> 68.3 us  [local(): pl.pallas_call(kernel, out_shape=(pltpu.VMEM((B, B, KT * 128), F32), pltp...]
where the time goes in v5:
time: 71 us; the launch traced here: 70.8 us
  Pallas kernels  68.3 us (96%)
  local copies, waits for them, and re-layouts  1.85 us (3%)
    pallas_call x1, Pallas kernels, local(): pl.pallas_call(kernel, out_shape=(pltpu.VMEM((B, B, KT * 128), F32), pltp...  68.3 us
    unnamed x2, local copies, waits for them, and re-layouts  1.85 us

profile of v5, /device:TPU:1, one launch (start us, length us, event | category | flops | bytes accessed | tf_op | source)
XLA Modules:
  0.0 70.8 jit_solution(5414988289945566010)
XLA Ops:
  0.6 68.3 %shard_map.95 = (f32[8,8,1024]{2,1,0:T(8,128)S(1)}, f32[3,8,128,128]{3,2,1,0:T(8,128)S(1)}) custom-call(f32[8,8,1024]{2,1,0:T(8,128)} %x0_hbm.1, f32[8,8,1024]{2,1,0:T(8,128)} %k_hbm.1, f32[8,8,1024]{2,1,0:T(8,128)} %c_hbm.1, f32[8,8,1024]{2,1,0:T(8,128)} %f_hbm.1, f32[3,8,8,1024]{3,2,1,0:T(8,128)} %u_hbm.1, s32[8,128]{1,0:T(8,128)} %lab.1, f32[2,2]{1,0:T(2,128)} %table.1, ...), custom_call_target="tpu_custom_call" | custom-call | tf_op jit(solution)/shard_map/pallas_call | solution.py:611
  68.9 0.7 copy.12
  69.6 1.1 %copy.13 = f32[3,8,128,128]{3,2,1,0:T(8,128)} copy(f32[3,8,128,128]{3,2,1,0:T(8,128)S(1)} %get-tuple-element.3) | data formatting | bytes 3145728
